TPU v7x, 32 devices: a whole 2x2x4 slice. The times are simulated.
32 devices in a mesh: energy: 8 (over y, x, core), atom: 4 (over z).
Axes of the slice: x: 2, y: 2, z: 4, core: 2. Of those that a mesh axis runs over, the one named last changes fastest.
Arguments:
- green_ret: bfloat16 [2, 12, 12, 384, 128], P(None, None, None, ('energy', 'atom')), may hold values from -1.59375 to 1.59375
- broadening: bfloat16 [2, 2, 12, 12, 384, 128], P(None, None, None, None, ('energy', 'atom')), may hold values from -6 to 6
- coupling: float32 [64], replicated, may hold values from 0.01 to 0.1
- occupation: float32 [64], replicated, may hold values from 0.05 to 3
- shifts: int32 [64], replicated, may hold values from 1 to 2, as said below
- neighbours: int32 [128, 34], P('atom'), may hold values from -24 to 151, as said below
- bond_count: int32 [128], P('atom'), may hold values from 17 to 34
- bond_weight: bfloat16 [128, 34], P('atom'), may hold values from -1 to 1
Outputs:
- self_energy: bfloat16 [2, 2, 12, 12, 384, 128], P(None, None, None, None, ('energy', 'atom'))
- polarization: float32 [64, 128], P('energy', 'atom')
Inputs may be any that keep to these rules, and one draw needn't show every extreme that they name: `shifts`: each mode's energy in energy steps. `neighbours`: the entries of row a are distinct and lie within 24 of a; entries outside 0 .. 127 name no atom. `bond_count`: the live slots of an atom are the leading ones of its row.
All inputs are finite; a program needn't handle non-finite values.
Results may differ from a plain program's by a relative error of at most 0.0076.
Values may be sent and summed in bfloat16 or wider, within the bound.
A program may use at most 128 MiB of HBM per device.

v0:
```python
import functools
import math

import jax
import jax.numpy as jnp
from jax import lax
from jax.experimental import pallas as pl
from jax.experimental.pallas import tpu as pltpu
from jax.sharding import PartitionSpec as P

SHIFT = 2
LANES = 128
ROWS = 8
IBLOCK = 3
JBLOCK = 4
MESH = pl.DeviceIdType.MESH


def ceil_to(value, step):
    return -(-value // step) * step


def pieces(first, count):
    parts, done = [], 0
    while done < count:
        tile, row = divmod(first + done, ROWS)
        size = min(ROWS - row, count - done)
        parts.append((tile, row, size, done))
        done += size
    return parts


def kernel(
    ne, nz, orb, energies, atoms, modes, slots,
    green, broad, coupling, occupation, shifts, count, neighbours, weight,
    out, pol,
    gv, sv, gf, sf, hf, ext, edge, send, recv, bonds, mixing, first, second,
    g_sem, s_sem, send_sem, recv_sem, bsend, brecv, fsend, frecv, ssend, srecv,
):
    e = lax.axis_index("energy")
    z = lax.axis_index("atom")
    chunks = atoms // LANES
    tiles = pl.cdiv(2 * energies, ROWS)
    stride = ceil_to(energies + 2 * SHIFT, ROWS)
    out_rows = ceil_to(energies, ROWS)
    iblocks, jblocks = orb // IBLOCK, orb // JBLOCK
    tile_width = atoms // nz
    last = ne * nz - 1
    place = e * nz + z

    def at_place(index):
        return {"energy": index // nz, "atom": lax.rem(index, nz)}

    above = at_place(lax.rem(place + 1, ne * nz))
    below = at_place(lax.rem(place + last, ne * nz))

    def input_copies(lc):
        lanes = pl.ds(pl.multiple_of(lc * LANES, LANES), LANES)
        return (
            pltpu.make_async_copy(green.at[:, :, :, :, lanes], gv, g_sem),
            pltpu.make_async_copy(broad.at[:, :, :, :, :, lanes], sv, s_sem),
        )

    if chunks == 1:
        for copy in input_copies(0):
            copy.start()

    barrier = pltpu.get_barrier_semaphore()
    pl.semaphore_signal(barrier, inc=1, device_id=above, device_id_type=MESH)
    pl.semaphore_signal(barrier, inc=1, device_id=below, device_id_type=MESH)

    @pl.loop(1, nz)
    def _(step):
        target = {"energy": e, "atom": lax.rem(z + step, nz)}
        pl.semaphore_signal(barrier, inc=1, device_id=target, device_id_type=MESH)

    @pl.loop(1, ne)
    def _(step):
        target = {"energy": lax.rem(e + step, ne), "atom": z}
        pl.semaphore_signal(barrier, inc=1, device_id=target, device_id_type=MESH)

    row_id = lax.broadcasted_iota(jnp.int32, (tile_width, slots), 0)
    slot_id = lax.broadcasted_iota(jnp.int32, (tile_width, slots), 1)
    live = jnp.zeros((tile_width, slots), jnp.int32)
    for row in range(tile_width):
        live = jnp.where(row_id == row, count[row], live)
    live_weight = jnp.where(slot_id < live, weight[...].astype(jnp.float32), 0.0)
    named = neighbours[...]
    atom_id = lax.broadcasted_iota(jnp.int32, (tile_width, atoms), 1)
    bond_rows = jnp.zeros((tile_width, atoms), jnp.float32)
    for slot in range(slots):
        bond_rows += jnp.where(
            named[:, slot : slot + 1] == atom_id, live_weight[:, slot : slot + 1], 0.0
        )
    bonds[z] = bond_rows.astype(jnp.bfloat16)

    def add_mode(q, sums):
        strength, filling, shift = coupling[q], occupation[q], shifts[q]
        emit, absorb = strength * (filling + 1.0), strength * filling
        return tuple(
            total + jnp.where(shift == level, term, 0.0)
            for level, (pair) in enumerate(zip(sums[::2], sums[1::2]), 1)
            for total, term in zip(pair, (emit, absorb))
        )

    sums = lax.fori_loop(0, modes, add_mode, (jnp.float32(0.0),) * (2 * SHIFT))
    rounded = [
        jnp.full((out_rows, LANES), total, jnp.float32).astype(jnp.bfloat16).astype(jnp.float32)
        for total in sums
    ]
    emission, absorption = rounded[::2], rounded[1::2]

    pl.semaphore_wait(barrier, 2 + (nz - 1) + (ne - 1))

    def bond_copy(step):
        return pltpu.make_async_remote_copy(
            src_ref=bonds.at[z],
            dst_ref=bonds.at[z],
            send_sem=bsend.at[step],
            recv_sem=brecv.at[step],
            device_id={"energy": e, "atom": lax.rem(z + step, nz)},
            device_id_type=MESH,
        )

    @pl.loop(1, nz)
    def _(step):
        bond_copy(step).start()

    def halo_copy(lc, ib, side):
        return pltpu.make_async_remote_copy(
            src_ref=send.at[lc, side, ib],
            dst_ref=recv.at[lc, side, ib],
            send_sem=send_sem.at[lc, side, ib],
            recv_sem=recv_sem.at[lc, side, ib],
            device_id=above if side else below,
            device_id_type=MESH,
        )

    def store_forms(target, index, forms):
        for form, value in enumerate(forms):
            for tile in range(tiles):
                low, high = tile * ROWS, min((tile + 1) * ROWS, 2 * energies)
                target[tile, form, index, :, 0 : high - low] = value[:, low:high]

    def keldysh_chunk(lc):
        g_copy, s_copy = input_copies(lc)
        if chunks > 1:
            g_copy.start()
            s_copy.start()
        g_copy.wait()

        @pl.loop(0, orb)
        def _(i):
            real = gv[0, i].astype(jnp.float32)
            imag = gv[1, i].astype(jnp.float32)
            real = jnp.concatenate([real, real], axis=1)
            imag = jnp.concatenate([imag, imag], axis=1)
            store_forms(gf, i, (real, imag, real + imag, real - imag))

        s_copy.wait()

        @pl.loop(0, orb)
        def _(i):
            real = [sv[k, 0, i].astype(jnp.float32) for k in range(2)]
            imag = [sv[k, 1, i].astype(jnp.float32) for k in range(2)]
            real = jnp.concatenate(real, axis=1)
            imag = jnp.concatenate(imag, axis=1)
            store_forms(sf, i, (real, imag, real + imag))

        @pl.loop(0, iblocks)
        def _(ib):
            irows = pl.ds(ib * IBLOCK, IBLOCK)

            @pl.loop(0, tiles * jblocks)
            def _(step):
                tile, jb = step // jblocks, lax.rem(step, jblocks)
                jrows = pl.ds(jb * JBLOCK, JBLOCK)
                total = [None] * 3
                for inner in range(orb):
                    for form in range(3):
                        term = gf[tile, form, irows, inner][:, None] * sf[tile, form, inner, jrows][None]
                        total[form] = term if inner == 0 else total[form] + term
                real = total[0] - total[1]
                imag = total[2] - total[0] - total[1]
                for form, value in enumerate((real, imag, real + imag)):
                    hf[tile, form, :, jrows] = value

            @pl.loop(0, jblocks)
            def _(jb):
                jrows = pl.ds(jb * JBLOCK, JBLOCK)
                for tile in range(tiles):
                    total = [None] * 3
                    for inner in range(orb):
                        for form, other in enumerate((0, 1, 3)):
                            term = hf[tile, form, :, inner][:, None] * gf[tile, other, jrows, inner][None]
                            total[form] = term if inner == 0 else total[form] + term
                    parts = (total[0] + total[1], total[2] - total[0] + total[1])
                    for c, value in enumerate(parts):
                        for k in range(2):
                            for t, row, size, done in pieces(k * energies, energies):
                                if t == tile:
                                    start = k * stride + SHIFT + done
                                    ext[lc, c, irows, jrows, start : start + size] = value[
                                        :, :, row : row + size
                                    ]
                            for side, begin in enumerate((0, energies - SHIFT)):
                                for t, row, size, done in pieces(k * energies + begin, SHIFT):
                                    if t == tile:
                                        for j in range(JBLOCK):
                                            start = (j * 2 + k) * SHIFT + done
                                            edge[side, c, :, jb, start : start + size] = value[
                                                :, j, row : row + size
                                            ]

            for side in range(2):
                send[lc, side, ib] = edge[side].astype(jnp.bfloat16)
                halo_copy(lc, ib, side).start()

    if chunks == 1:
        keldysh_chunk(0)
    else:
        pl.loop(0, chunks)(keldysh_chunk)

    @pl.loop(1, nz)
    def _(step):
        bond_copy(step).wait()

    for lc in range(chunks):
        block = bonds[:, :, lc * LANES : (lc + 1) * LANES].reshape(atoms, LANES)
        mixing[lc] = block.astype(jnp.float32).T.astype(jnp.bfloat16)

    keep_high = (place != last).astype(jnp.float32)
    keep_low = (place != 0).astype(jnp.float32)

    def halo_rows(lc):
        @pl.loop(0, iblocks)
        def _(ib):
            for side in range(2):
                halo_copy(lc, ib, side).wait()

            @pl.loop(0, 2 * IBLOCK)
            def _(step):
                c, i = step // IBLOCK, lax.rem(step, IBLOCK)
                for side, keep in enumerate((keep_high, keep_low)):
                    rows = recv[lc, side, ib, c, i].astype(jnp.float32) * keep
                    for k in range(2):
                        start = k * stride + (0 if side else SHIFT + energies)
                        for j in range(orb):
                            row = ((j % JBLOCK) * 2 + k) * SHIFT
                            ext[lc, c, ib * IBLOCK + i, j, start : start + SHIFT] = rows[
                                j // JBLOCK, row : row + SHIFT
                            ]

    if chunks == 1:
        halo_rows(0)
    else:
        pl.loop(0, chunks)(halo_rows)

    def traces(lc):
        def add_row(c, i, totals):
            ahead = ext[lc, c, i, :, SHIFT : SHIFT + energies]
            result = []
            for offset, total in enumerate(totals, 1):
                start = stride + SHIFT - offset
                term = jnp.sum(ahead * ext[lc, c, :, i, start : start + energies], axis=0)
                result.append(total - term if c else total + term)
            return tuple(result)

        totals = (jnp.zeros((energies, LANES), jnp.float32),) * SHIFT
        for c in range(2):
            totals = lax.fori_loop(0, orb, functools.partial(add_row, c), totals)
        first[0, lc] = jnp.zeros((ROWS, LANES), jnp.float32)
        for offset, total in enumerate(totals):
            first[0, lc, offset : offset + 1] = jnp.sum(total, axis=0, keepdims=True)

    if chunks == 1:
        traces(0)
    else:
        pl.loop(0, chunks)(traces)

    def first_copy(step):
        return pltpu.make_async_remote_copy(
            src_ref=first.at[0],
            dst_ref=first.at[step],
            send_sem=fsend.at[step],
            recv_sem=frecv.at[step],
            device_id={"energy": e, "atom": lax.rem(z + step, nz)},
            device_id_type=MESH,
        )

    def second_copy(step):
        return pltpu.make_async_remote_copy(
            src_ref=second.at[0],
            dst_ref=second.at[step],
            send_sem=ssend.at[step],
            recv_sem=srecv.at[step],
            device_id={"energy": lax.rem(e + step, ne), "atom": z},
            device_id_type=MESH,
        )

    def self_energy(c):
        @pl.loop(0, orb)
        def _(i):
            for k in range(2):
                upward, downward = (emission, absorption) if k == 0 else (absorption, emission)
                mixed = None
                for lc in range(chunks):
                    total = None
                    for offset in range(1, SHIFT + 1):
                        for sign, factor in ((1, upward[offset - 1]), (-1, downward[offset - 1])):
                            start = k * stride + SHIFT + sign * offset
                            term = factor[None] * ext[lc, c, i, :, start : start + out_rows]
                            total = term if total is None else total + term
                    flat = total.reshape(orb * out_rows, LANES).astype(jnp.bfloat16)
                    product = jnp.dot(flat, mixing[lc], preferred_element_type=jnp.float32)
                    mixed = product if mixed is None else mixed + product
                mixed = mixed.reshape(orb, out_rows, atoms)
                out[k, c, i] = mixed[:, :energies].astype(jnp.bfloat16)

    @pl.loop(1, nz)
    def _(step):
        first_copy(step).start()

    self_energy(0)

    @pl.loop(1, nz)
    def _(step):
        first_copy(step).wait()

    second[0] = jnp.sum(first[...], axis=0)

    @pl.loop(1, ne)
    def _(step):
        second_copy(step).start()

    self_energy(1)

    @pl.loop(1, ne)
    def _(step):
        second_copy(step).wait()

    summed = jnp.sum(second[...], axis=0)
    own = jnp.zeros((ROWS, tile_width), jnp.float32)
    for tile in range(nz):
        lc, lane = divmod(tile * tile_width, LANES)
        own = jnp.where(z == tile, summed[lc, :, lane : lane + tile_width], own)
    share = modes // ne
    scale = 1.0 / math.sqrt(energies * ne * nz)
    for row in range(share):
        mode = e * share + row
        shift = shifts[mode]
        line = jnp.zeros((1, tile_width), jnp.float32)
        for level in range(1, SHIFT + 1):
            line += jnp.where(shift == level, 1.0, 0.0) * own[level - 1 : level]
        pol[row : row + 1] = line * (coupling[mode] * scale)


def local(ne, nz, green_ret, broadening, coupling, occupation, shifts, neighbours, bond_count, bond_weight):
    orb, energies, atoms = green_ret.shape[1], green_ret.shape[3], green_ret.shape[4]
    modes, slots = coupling.shape[0], neighbours.shape[1]
    tile_width = neighbours.shape[0]
    chunks = atoms // LANES
    tiles = pl.cdiv(2 * energies, ROWS)
    stride = ceil_to(energies + 2 * SHIFT, ROWS)
    out_rows = ceil_to(energies, ROWS)
    ext_rows = ceil_to(stride + out_rows + 2 * SHIFT, ROWS)
    iblocks, jblocks = orb // IBLOCK, orb // JBLOCK
    edge_shape = (2, IBLOCK, jblocks, JBLOCK * 2 * SHIFT, LANES)
    halo_shape = (chunks, 2, iblocks) + edge_shape
    dma = pltpu.SemaphoreType.DMA
    vmem = pl.BlockSpec(memory_space=pltpu.VMEM)
    smem = pl.BlockSpec(memory_space=pltpu.SMEM)
    anywhere = pl.BlockSpec(memory_space=pl.ANY)
    call = pl.pallas_call(
        functools.partial(kernel, ne, nz, orb, energies, atoms, modes, slots),
        out_shape=(
            jax.ShapeDtypeStruct(broadening.shape, jnp.bfloat16),
            jax.ShapeDtypeStruct((modes // ne, tile_width), jnp.float32),
        ),
        in_specs=[anywhere, anywhere, smem, smem, smem, smem, vmem, vmem],
        out_specs=(vmem, vmem),
        scratch_shapes=[
            pltpu.VMEM((2, orb, orb, energies, LANES), jnp.bfloat16),
            pltpu.VMEM((2, 2, orb, orb, energies, LANES), jnp.bfloat16),
            pltpu.VMEM((tiles, 4, orb, orb, ROWS, LANES), jnp.float32),
            pltpu.VMEM((tiles, 3, orb, orb, ROWS, LANES), jnp.float32),
            pltpu.VMEM((tiles, 3, IBLOCK, orb, ROWS, LANES), jnp.float32),
            pltpu.VMEM((chunks, 2, orb, orb, ext_rows, LANES), jnp.float32),
            pltpu.VMEM((2,) + edge_shape, jnp.float32),
            pltpu.VMEM(halo_shape, jnp.bfloat16),
            pltpu.VMEM(halo_shape, jnp.bfloat16),
            pltpu.VMEM((nz, tile_width, atoms), jnp.bfloat16),
            pltpu.VMEM((chunks, LANES, atoms), jnp.bfloat16),
            pltpu.VMEM((nz, chunks, ROWS, LANES), jnp.float32),
            pltpu.VMEM((ne, chunks, ROWS, LANES), jnp.float32),
            dma,
            dma,
            dma((chunks, 2, iblocks)),
            dma((chunks, 2, iblocks)),
            dma((nz,)),
            dma((nz,)),
            dma((nz,)),
            dma((nz,)),
            dma((ne,)),
            dma((ne,)),
        ],
        compiler_params=pltpu.CompilerParams(
            collective_id=0, has_side_effects=True, vmem_limit_bytes=60 * 1024 * 1024
        ),
    )
    return call(green_ret, broadening, coupling, occupation, shifts, bond_count, neighbours, bond_weight)


def solution(mesh):
    in_specs = (
        P(None, None, None, ("energy", "atom"), None),
        P(None, None, None, None, ("energy", "atom"), None),
        P(),
        P(),
        P(),
        P("atom", None),
        P("atom"),
        P("atom", None),
    )
    out_specs = (P(None, None, None, None, ("energy", "atom"), None), P("energy", "atom"))
    body = functools.partial(local, mesh.shape["energy"], mesh.shape["atom"])
    return jax.shard_map(body, mesh=mesh, in_specs=in_specs, out_specs=out_specs, check_vma=False)
```

profile of v0, /device:TPU:0, one launch (start us, length us, event | category | flops | bytes accessed | tf_op | source)
XLA Modules:
  0.0 45.0 jit_solution(14361871428334762016)
XLA Ops:
  0.6 0.0 copy-start
  0.6 2.6 %copy.10.green = bf16[2,12,12,12,128]{4,3,2,1,0:T(8,128)(2,1)} copy(bf16[2,12,12,12,128]{4,0,3,2,1:T(2,128)(2,1)} %param.8) | data formatting | bytes 1769472 | tf_op args[0]
  3.2 0.0 copy-done
  3.2 2.0 %copy.11.broad = bf16[2,2,12,12,12,128]{5,4,3,2,1,0:T(8,128)(2,1)} copy(bf16[2,2,12,12,12,128]{5,1,4,3,2,0:T(2,128)(2,1)S(1)} %copy-done) | data formatting | bytes 3538944 | tf_op args[1]
  5.2 33.6 %shard_map.95 = (bf16[2,2,12,12,12,128]{5,4,3,2,1,0:T(8,128)(2,1)}, f32[8,32]{1,0:T(8,128)}) custom-call(bf16[2,12,12,12,128]{4,3,2,1,0:T(8,128)(2,1)} %copy.10.green, bf16[2,2,12,12,12,128]{5,4,3,2,1,0:T(8,128)(2,1)} %copy.11.broad, f32[64]{0:T(128)} %coupling.1, f32[64]{0:T(128)} %occupation.1, s32[64]{0:T(128)} %shifts.1, s32[32]{0:T(128)} %count.1, ...), custom_call_target="tpu_custom_call" | custom-call | tf_op jit(solution)/shard_map/pallas_call | solution.py:411
  38.8 0.0 copy-start.1
  38.8 5.6 %copy.12 = bf16[2,2,12,12,12,128]{5,1,4,3,2,0:T(2,128)(2,1)} copy(bf16[2,2,12,12,12,128]{5,4,3,2,1,0:T(8,128)(2,1)} %get-tuple-element.2) | data formatting | bytes 3538944 | tf_op jit(solution)/shard_map/pallas_call | solution.py:411
  44.4 0.0 copy-done.1
  44.4 0.6 %copy.14 = f32[8,32]{1,0:T(8,128)} copy(f32[8,32]{1,0:T(8,128)S(1)} %copy-done.1) | data formatting | bytes 2048
Async XLA Ops:
  0.6 2.6 %copy-start = (bf16[2,2,12,12,12,128]{5,1,4,3,2,0:T(2,128)(2,1)S(1)}, bf16[2,2,12,12,12,128]{5,1,4,3,2,0:T(2,128)(2,1)}, u32[]{:S(2)}) copy-start(bf16[2,2,12,12,12,128]{5,1,4,3,2,0:T(2,128)(2,1)} %param.9) | copy-start | bytes 5308420
  38.8 5.6 %copy-start.1 = (f32[8,32]{1,0:T(8,128)S(1)}, f32[8,32]{1,0:T(8,128)}, u32[]{:S(2)}) copy-start(f32[8,32]{1,0:T(8,128)} %get-tuple-element.7) | copy-start | bytes 3076
where the time goes:
time: 45.2 us; the launch traced here: 45 us
  Pallas kernels  33.6 us (74%)
  local copies, waits for them, and re-layouts  10.8 us (24%)
  between operations  0.66 us (1%)
    pallas_call x1, Pallas kernels, local(): call(green_ret, broadening, coupling, occupation, shifts, bond_count, nei...  33.6 us
    pallas_call x1, local copies, waits for them, and re-layouts, local(): call(green_ret, broadening, coupling, occupation, shifts, bond_count, nei...  5.61 us
    unnamed x7, local copies, waits for them, and re-layouts  5.15 us

commit v1 on v0

v1 whole, which is shorter than its diff:
```python
import functools
import math

import jax
import jax.numpy as jnp
from jax import lax
from jax.experimental import pallas as pl
from jax.experimental.pallas import tpu as pltpu
from jax.sharding import PartitionSpec as P

SHIFT = 2
LANES = 128
ROWS = 8
IBLOCK = 3
JBLOCK = 4
MESH = pl.DeviceIdType.MESH


def ceil_to(value, step):
    return -(-value // step) * step


def pieces(first, count):
    parts, done = [], 0
    while done < count:
        tile, row = divmod(first + done, ROWS)
        size = min(ROWS - row, count - done)
        parts.append((tile, row, size, done))
        done += size
    return parts


def keldysh_kernel(
    ne, nz, orb, energies, atoms, modes, slots,
    green, broad, coupling, occupation, shifts, count, neighbours, weight,
    shifted, mixing, summed,
    gv, sv, plain, gf, sf, hf, ext, edge, send, recv, bonds, first, second,
    g_sem, s_sem, send_sem, recv_sem, bsend, brecv, fsend, frecv, ssend, srecv,
):
    e = lax.axis_index("energy")
    z = lax.axis_index("atom")
    chunks = atoms // LANES
    pair_rows = 2 * energies
    tiles = pl.cdiv(pair_rows, ROWS)
    halo = 2 * SHIFT
    out_rows = ceil_to(pair_rows, ROWS)
    iblocks, jblocks = orb // IBLOCK, orb // JBLOCK
    tile_width = atoms // nz
    last = ne * nz - 1
    place = e * nz + z

    def at_place(index):
        return {"energy": index // nz, "atom": lax.rem(index, nz)}

    above = at_place(lax.rem(place + 1, ne * nz))
    below = at_place(lax.rem(place + last, ne * nz))

    def input_copies(lc):
        lanes = pl.ds(pl.multiple_of(lc * LANES, LANES), LANES)
        return (
            pltpu.make_async_copy(green.at[:, :, :, lanes], gv, g_sem),
            pltpu.make_async_copy(broad.at[:, :, :, :, lanes], sv, s_sem),
        )

    if chunks == 1:
        for copy in input_copies(0):
            copy.start()

    barrier = pltpu.get_barrier_semaphore()
    pl.semaphore_signal(barrier, inc=1, device_id=above, device_id_type=MESH)
    pl.semaphore_signal(barrier, inc=1, device_id=below, device_id_type=MESH)

    @pl.loop(1, nz)
    def _(step):
        target = {"energy": e, "atom": lax.rem(z + step, nz)}
        pl.semaphore_signal(barrier, inc=1, device_id=target, device_id_type=MESH)

    @pl.loop(1, ne)
    def _(step):
        target = {"energy": lax.rem(e + step, ne), "atom": z}
        pl.semaphore_signal(barrier, inc=1, device_id=target, device_id_type=MESH)

    row_id = lax.broadcasted_iota(jnp.int32, (tile_width, slots), 0)
    slot_id = lax.broadcasted_iota(jnp.int32, (tile_width, slots), 1)
    live = jnp.zeros((tile_width, slots), jnp.int32)
    for row in range(tile_width):
        live = jnp.where(row_id == row, count[row], live)
    live_weight = jnp.where(slot_id < live, weight[...].astype(jnp.float32), 0.0)
    named = neighbours[...]
    atom_id = lax.broadcasted_iota(jnp.int32, (tile_width, atoms), 1)
    bond_rows = jnp.zeros((tile_width, atoms), jnp.float32)
    for slot in range(slots):
        bond_rows += jnp.where(
            named[:, slot : slot + 1] == atom_id, live_weight[:, slot : slot + 1], 0.0
        )
    bonds[z] = bond_rows.astype(jnp.bfloat16)

    def add_mode(q, sums):
        strength, filling, shift = coupling[q], occupation[q], shifts[q]
        emit, absorb = strength * (filling + 1.0), strength * filling
        return tuple(
            total + jnp.where(shift == level, term, 0.0)
            for level, pair in enumerate(zip(sums[::2], sums[1::2]), 1)
            for total, term in zip(pair, (emit, absorb))
        )

    sums = lax.fori_loop(0, modes, add_mode, (jnp.float32(0.0),) * (2 * SHIFT))
    rounded = [
        jnp.full((out_rows, LANES), total, jnp.float32).astype(jnp.bfloat16).astype(jnp.float32)
        for total in sums
    ]
    emission, absorption = rounded[::2], rounded[1::2]

    def bond_copy(step):
        return pltpu.make_async_remote_copy(
            src_ref=bonds.at[z],
            dst_ref=bonds.at[z],
            send_sem=bsend.at[step],
            recv_sem=brecv.at[step],
            device_id={"energy": e, "atom": lax.rem(z + step, nz)},
            device_id_type=MESH,
        )

    def halo_copy(lc, ib, side):
        return pltpu.make_async_remote_copy(
            src_ref=send.at[lc, side, ib],
            dst_ref=recv.at[lc, side, ib],
            send_sem=send_sem.at[lc, side, ib],
            recv_sem=recv_sem.at[lc, side, ib],
            device_id=above if side else below,
            device_id_type=MESH,
        )

    def store_forms(target, index, count_of):
        for tile in range(tiles):
            low = tile * ROWS
            size = min(ROWS, pair_rows - low)
            real = plain[:, pl.ds(2 * low, size, stride=2)]
            imag = plain[:, pl.ds(2 * low + 1, size, stride=2)]
            forms = (real, imag, real + imag, real - imag)
            for form in range(count_of):
                target[tile, form, index, :, 0:size] = forms[form]

    def prepare(lc):
        g_copy, s_copy = input_copies(lc)
        if chunks > 1:
            g_copy.start()
            s_copy.start()
        g_copy.wait()

        @pl.loop(0, orb)
        def _(i):
            block = gv[i].astype(jnp.float32)
            plain[:, 0:pair_rows] = block
            plain[:, pair_rows : 2 * pair_rows] = block
            store_forms(gf, i, 4)

        s_copy.wait()

        @pl.loop(0, orb)
        def _(i):
            for k in range(2):
                plain[:, k * pair_rows : (k + 1) * pair_rows] = sv[k, i].astype(jnp.float32)
            store_forms(sf, i, 3)

    def keldysh_chunk(lc):
        if chunks > 1:
            prepare(lc)

        @pl.loop(0, iblocks)
        def _(ib):
            irows = pl.ds(ib * IBLOCK, IBLOCK)

            @pl.loop(0, tiles * jblocks)
            def _(step):
                tile, jb = step // jblocks, lax.rem(step, jblocks)
                jrows = pl.ds(jb * JBLOCK, JBLOCK)
                total = [None] * 3
                for inner in range(orb):
                    for form in range(3):
                        term = gf[tile, form, irows, inner][:, None] * sf[tile, form, inner, jrows][None]
                        total[form] = term if inner == 0 else total[form] + term
                real = total[0] - total[1]
                imag = total[2] - total[0] - total[1]
                for form, value in enumerate((real, imag, real + imag)):
                    hf[tile, form, :, jrows] = value

            @pl.loop(0, jblocks)
            def _(jb):
                jrows = pl.ds(jb * JBLOCK, JBLOCK)
                for tile in range(tiles):
                    total = [None] * 3
                    for inner in range(orb):
                        for form, other in enumerate((0, 1, 3)):
                            term = hf[tile, form, :, inner][:, None] * gf[tile, other, jrows, inner][None]
                            total[form] = term if inner == 0 else total[form] + term
                    parts = (total[0] + total[1], total[2] - total[0] + total[1])
                    for c, value in enumerate(parts):
                        for k in range(2):
                            for t, row, size, done in pieces(k * energies, energies):
                                if t == tile:
                                    start = halo + 2 * done + c
                                    ext[lc, k, irows, jrows, pl.ds(start, size, stride=2)] = value[
                                        :, :, row : row + size
                                    ]

            for side, start in enumerate((halo, pair_rows)):
                for k in range(2):
                    for j in range(orb):
                        row = (j % JBLOCK) * halo
                        edge[side, k, :, j // JBLOCK, row : row + halo] = ext[
                            lc, k, irows, j, start : start + halo
                        ]
                send[lc, side, ib] = edge[side].astype(jnp.bfloat16)
                halo_copy(lc, ib, side).start()

    if chunks == 1:
        prepare(0)
    pl.semaphore_wait(barrier, 2 + (nz - 1) + (ne - 1))

    @pl.loop(1, nz)
    def _(step):
        bond_copy(step).start()

    if chunks == 1:
        keldysh_chunk(0)
    else:
        pl.loop(0, chunks)(keldysh_chunk)

    def inner_traces(lc):
        def add_row(i, totals):
            result = []
            for offset, total in enumerate(totals, 1):
                size = pair_rows - 2 * offset
                ahead = ext[lc, 0, i, :, halo + 2 * offset : halo + pair_rows]
                behind = ext[lc, 1, :, i, halo : halo + size]
                result.append(total + jnp.sum(ahead * behind, axis=0))
            return tuple(result)

        starts = tuple(
            jnp.zeros((pair_rows - 2 * offset, LANES), jnp.float32)
            for offset in range(1, SHIFT + 1)
        )
        return lax.fori_loop(0, orb, add_row, starts)

    def signed_sum(total):
        parity = lax.rem(lax.broadcasted_iota(jnp.int32, total.shape, 0), 2)
        return jnp.sum(jnp.where(parity == 0, total, -total), axis=0, keepdims=True)

    def store_inner(lc):
        first[0, lc] = jnp.zeros((ROWS, LANES), jnp.float32)
        for offset, total in enumerate(inner_traces(lc)):
            if total.shape[0]:
                first[0, lc, offset : offset + 1] = signed_sum(total)

    if chunks == 1:
        store_inner(0)
    else:
        pl.loop(0, chunks)(store_inner)

    @pl.loop(1, nz)
    def _(step):
        bond_copy(step).wait()

    for lc in range(chunks):
        block = bonds[:, :, lc * LANES : (lc + 1) * LANES].reshape(atoms, LANES)
        mixing[lc] = block.astype(jnp.float32).T.astype(jnp.bfloat16)

    keep_high = (place != last).astype(jnp.float32)
    keep_low = (place != 0).astype(jnp.float32)

    def halo_rows(lc):
        def take_block(ib, totals):
            for side in range(2):
                halo_copy(lc, ib, side).wait()
            irows = pl.ds(ib * IBLOCK, IBLOCK)
            for side, keep in enumerate((keep_high, keep_low)):
                start = 0 if side else halo + pair_rows
                for k in range(2):
                    rows = recv[lc, side, ib, k].astype(jnp.float32) * keep
                    for j in range(orb):
                        row = (j % JBLOCK) * halo
                        ext[lc, k, irows, j, start : start + halo] = rows[
                            :, j // JBLOCK, row : row + halo
                        ]
            totals = list(totals)
            for step in range(IBLOCK):
                i = ib * IBLOCK + step
                for offset in range(1, SHIFT + 1):
                    ahead = ext[lc, 0, :, i, halo : halo + 2 * offset]
                    behind = ext[lc, 1, i, :, halo - 2 * offset : halo]
                    totals[offset - 1] += jnp.sum(ahead * behind, axis=0)
            return tuple(totals)

        starts = tuple(
            jnp.zeros((2 * offset, LANES), jnp.float32) for offset in range(1, SHIFT + 1)
        )
        totals = lax.fori_loop(0, iblocks, take_block, starts)
        for offset, total in enumerate(totals):
            first[0, lc, offset : offset + 1] += signed_sum(total)

    if chunks == 1:
        halo_rows(0)
    else:
        pl.loop(0, chunks)(halo_rows)

    def first_copy(step):
        return pltpu.make_async_remote_copy(
            src_ref=first.at[0],
            dst_ref=first.at[step],
            send_sem=fsend.at[step],
            recv_sem=frecv.at[step],
            device_id={"energy": e, "atom": lax.rem(z + step, nz)},
            device_id_type=MESH,
        )

    def second_copy(step):
        return pltpu.make_async_remote_copy(
            src_ref=second.at[0],
            dst_ref=second.at[step],
            send_sem=ssend.at[step],
            recv_sem=srecv.at[step],
            device_id={"energy": lax.rem(e + step, ne), "atom": z},
            device_id_type=MESH,
        )

    def shift_energies(k):
        upward, downward = (emission, absorption) if k == 0 else (absorption, emission)

        @pl.loop(0, chunks * orb)
        def _(step):
            lc, i = step // orb, lax.rem(step, orb)
            total = None
            for offset in range(1, SHIFT + 1):
                for sign, factor in ((1, upward[offset - 1]), (-1, downward[offset - 1])):
                    start = halo + 2 * sign * offset
                    term = factor[None] * ext[lc, k, i, :, start : start + out_rows]
                    total = term if total is None else total + term
            flat = total.reshape(orb * out_rows, LANES)
            shifted[k, lc, i] = flat.astype(jnp.bfloat16)

    @pl.loop(1, nz)
    def _(step):
        first_copy(step).start()

    shift_energies(0)

    @pl.loop(1, nz)
    def _(step):
        first_copy(step).wait()

    second[0] = jnp.sum(first[...], axis=0)

    @pl.loop(1, ne)
    def _(step):
        second_copy(step).start()

    shift_energies(1)

    @pl.loop(1, ne)
    def _(step):
        second_copy(step).wait()

    summed[...] = jnp.sum(second[...], axis=0)


def mixing_kernel(ne, nz, orb, energies, atoms, modes, coupling, shifts, shifted, mixing, summed, out, pol):
    chunks = atoms // LANES
    pair_rows = 2 * energies
    out_rows = ceil_to(pair_rows, ROWS)
    for row in range(IBLOCK):
        mixed = None
        for lc in range(chunks):
            product = jnp.dot(
                shifted[0, lc, row], mixing[lc], preferred_element_type=jnp.float32
            )
            mixed = product if mixed is None else mixed + product
        mixed = mixed.reshape(orb, out_rows, atoms)
        out[0, row] = mixed[:, :pair_rows].astype(jnp.bfloat16)

    @pl.when((pl.program_id(0) == 0) & (pl.program_id(1) == 0))
    def _():
        e = lax.axis_index("energy")
        z = lax.axis_index("atom")
        tile_width = atoms // nz
        own = jnp.zeros((ROWS, tile_width), jnp.float32)
        for tile in range(nz):
            lc, lane = divmod(tile * tile_width, LANES)
            own = jnp.where(z == tile, summed[lc, :, lane : lane + tile_width], own)
        share = modes // ne
        scale = 1.0 / math.sqrt(energies * ne * nz)
        for row in range(share):
            mode = e * share + row
            shift = shifts[mode]
            line = jnp.zeros((1, tile_width), jnp.float32)
            for level in range(1, SHIFT + 1):
                line += jnp.where(shift == level, 1.0, 0.0) * own[level - 1 : level]
            pol[row : row + 1] = line * (coupling[mode] * scale)


def local(ne, nz, green_ret, broadening, coupling, occupation, shifts, neighbours, bond_count, bond_weight):
    orb, energies, atoms = green_ret.shape[1], green_ret.shape[3], green_ret.shape[4]
    modes, slots = coupling.shape[0], neighbours.shape[1]
    tile_width = neighbours.shape[0]
    chunks = atoms // LANES
    pair_rows = 2 * energies
    tiles = pl.cdiv(pair_rows, ROWS)
    out_rows = ceil_to(pair_rows, ROWS)
    ext_rows = ceil_to(max(pair_rows, out_rows) + 4 * SHIFT, ROWS)
    iblocks, jblocks = orb // IBLOCK, orb // JBLOCK
    edge_shape = (2, IBLOCK, jblocks, JBLOCK * 2 * SHIFT, LANES)
    halo_shape = (chunks, 2, iblocks) + edge_shape
    dma = pltpu.SemaphoreType.DMA
    vmem = pl.BlockSpec(memory_space=pltpu.VMEM)
    smem = pl.BlockSpec(memory_space=pltpu.SMEM)
    anywhere = pl.BlockSpec(memory_space=pl.ANY)
    green = green_ret.transpose(1, 2, 3, 0, 4).reshape(orb, orb, pair_rows, atoms)
    broad = broadening.transpose(0, 2, 3, 4, 1, 5).reshape(2, orb, orb, pair_rows, atoms)
    shifted, mixing, summed = pl.pallas_call(
        functools.partial(keldysh_kernel, ne, nz, orb, energies, atoms, modes, slots),
        out_shape=(
            jax.ShapeDtypeStruct((2, chunks, orb, orb * out_rows, LANES), jnp.bfloat16),
            jax.ShapeDtypeStruct((chunks, LANES, atoms), jnp.bfloat16),
            jax.ShapeDtypeStruct((chunks, ROWS, LANES), jnp.float32),
        ),
        in_specs=[anywhere, anywhere, smem, smem, smem, smem, vmem, vmem],
        out_specs=(vmem, vmem, vmem),
        scratch_shapes=[
            pltpu.VMEM((orb, orb, pair_rows, LANES), jnp.bfloat16),
            pltpu.VMEM((2, orb, orb, pair_rows, LANES), jnp.bfloat16),
            pltpu.VMEM((orb, 2 * pair_rows, LANES), jnp.float32),
            pltpu.VMEM((tiles, 4, orb, orb, ROWS, LANES), jnp.float32),
            pltpu.VMEM((tiles, 3, orb, orb, ROWS, LANES), jnp.float32),
            pltpu.VMEM((tiles, 3, IBLOCK, orb, ROWS, LANES), jnp.float32),
            pltpu.VMEM((chunks, 2, orb, orb, ext_rows, LANES), jnp.float32),
            pltpu.VMEM((2,) + edge_shape, jnp.float32),
            pltpu.VMEM(halo_shape, jnp.bfloat16),
            pltpu.VMEM(halo_shape, jnp.bfloat16),
            pltpu.VMEM((nz, tile_width, atoms), jnp.bfloat16),
            pltpu.VMEM((nz, chunks, ROWS, LANES), jnp.float32),
            pltpu.VMEM((ne, chunks, ROWS, LANES), jnp.float32),
            dma,
            dma,
            dma((chunks, 2, iblocks)),
            dma((chunks, 2, iblocks)),
            dma((nz,)),
            dma((nz,)),
            dma((nz,)),
            dma((nz,)),
            dma((ne,)),
            dma((ne,)),
        ],
        compiler_params=pltpu.CompilerParams(
            collective_id=0, has_side_effects=True, vmem_limit_bytes=48 * 1024 * 1024
        ),
    )(green, broad, coupling, occupation, shifts, bond_count, neighbours, bond_weight)
    out, pol = pl.pallas_call(
        functools.partial(mixing_kernel, ne, nz, orb, energies, atoms, modes),
        grid=(2, iblocks),
        out_shape=(
            jax.ShapeDtypeStruct((2, orb, orb, pair_rows, atoms), jnp.bfloat16),
            jax.ShapeDtypeStruct((modes // ne, tile_width), jnp.float32),
        ),
        in_specs=[
            smem,
            smem,
            pl.BlockSpec((1, chunks, IBLOCK, orb * out_rows, LANES), lambda k, ib: (k, 0, ib, 0, 0)),
            pl.BlockSpec((chunks, LANES, atoms), lambda k, ib: (0, 0, 0)),
            pl.BlockSpec((chunks, ROWS, LANES), lambda k, ib: (0, 0, 0)),
        ],
        out_specs=(
            pl.BlockSpec((1, IBLOCK, orb, pair_rows, atoms), lambda k, ib: (k, ib, 0, 0, 0)),
            pl.BlockSpec((modes // ne, tile_width), lambda k, ib: (0, 0)),
        ),
        compiler_params=pltpu.CompilerParams(vmem_limit_bytes=24 * 1024 * 1024),
    )(coupling, shifts, shifted, mixing, summed)
    self_energy = out.reshape(2, orb, orb, energies, 2, atoms).transpose(0, 4, 1, 2, 3, 5)
    return self_energy, pol


def solution(mesh):
    in_specs = (
        P(None, None, None, ("energy", "atom"), None),
        P(None, None, None, None, ("energy", "atom"), None),
        P(),
        P(),
        P(),
        P("atom", None),
        P("atom"),
        P("atom", None),
    )
    out_specs = (P(None, None, None, None, ("energy", "atom"), None), P("energy", "atom"))
    body = functools.partial(local, mesh.shape["energy"], mesh.shape["atom"])
    return jax.shard_map(body, mesh=mesh, in_specs=in_specs, out_specs=out_specs, check_vma=False)
```

time: 45.2 us -> 44.1 us (0.976)
  local copies, waits for them, and re-layouts: 10.8 us -> 6.67 us
  Pallas kernels: 33.6 us -> 36.5 us
    pallas_call x1 -> x0, local copies, waits for them, and re-layouts: 5.61 us -> none  [local(): call(green_ret, broadening, coupling, occupation, shifts, bond_count, nei...]
    pallas_call x1 -> x2, Pallas kernels: 33.6 us -> 36.5 us  [the longest x1 31.7 us: local(): pl.pallas_call(functools.partial(keldysh_kernel, ne, nz, orb, energies, a...]
    unnamed x7 -> x16, local copies, waits for them, and re-layouts: 5.15 us -> 6.67 us
where the time goes in v1:
time: 44.1 us; the launch traced here: 43.8 us
  Pallas kernels  36.5 us (83%)
  local copies, waits for them, and re-layouts  6.67 us (15%)
  between operations  0.66 us (1%)
    pallas_call x1, Pallas kernels, local(): pl.pallas_call(functools.partial(keldysh_kernel, ne, nz, orb, energies, a...  31.7 us
    unnamed x16, local copies, waits for them, and re-layouts  6.67 us
    pallas_call x1, Pallas kernels, local(): pl.pallas_call(functools.partial(mixing_kernel, ne, nz, orb, energies, at...  4.71 us

profile of v1, /device:TPU:0, one launch (start us, length us, event | category | flops | bytes accessed | tf_op | source)
XLA Modules:
  0.0 43.8 jit_solution(8265679974075758143)
XLA Ops:
  0.6 0.0 copy-start
  0.6 1.5 %copy-done = bf16[2,2,12,12,12,128]{5,1,4,3,2,0:T(2,128)(2,1)S(1)} copy-done((bf16[2,2,12,12,12,128]{5,1,4,3,2,0:T(2,128)(2,1)S(1)}, bf16[2,2,12,12,12,128]{5,1,4,3,2,0:T(2,128)(2,1)}, u32[]{:S(2)}) %copy-start) | copy-done | bytes 1769496
  2.1 0.0 copy-start.1
  2.1 1.2 %copy-done.1 = bf16[2,12,12,12,128]{4,0,3,2,1:T(2,128)(2,1)S(1)} copy-done((bf16[2,12,12,12,128]{4,0,3,2,1:T(2,128)(2,1)S(1)}, bf16[2,12,12,12,128]{4,0,3,2,1:T(2,128)(2,1)}, u32[]{:S(2)}) %copy-start.1) | copy-done | bytes 884760
  3.3 0.0 copy-start.2
  3.3 0.7 %copy-done.2 = s32[32,34]{1,0:T(8,128)S(1)} copy-done((s32[32,34]{1,0:T(8,128)S(1)}, s32[32,34]{1,0:T(8,128)}, u32[]{:S(2)}) %copy-start.2) | copy-done | bytes 4376
  4.0 0.0 copy-start.3
  4.0 0.7 %copy-done.3 = bf16[32,34]{1,0:T(8,128)(2,1)S(1)} copy-done((bf16[32,34]{1,0:T(8,128)(2,1)S(1)}, bf16[32,34]{1,0:T(8,128)(2,1)}, u32[]{:S(2)}) %copy-start.3) | copy-done | bytes 2200
  4.7 0.0 copy-start.4
  4.7 0.7 %copy-done.4 = f32[64]{0:T(128)S(1)} copy-done((f32[64]{0:T(128)S(1)}, f32[64]{0:T(128)}, u32[]{:S(2)}) %copy-start.4) | copy-done | bytes 280
  5.3 0.0 copy-start.5
  5.4 0.7 %copy-done.5 = s32[64]{0:T(128)S(1)} copy-done((s32[64]{0:T(128)S(1)}, s32[64]{0:T(128)}, u32[]{:S(2)}) %copy-start.5) | copy-done | bytes 280
  6.0 0.0 copy-start.6
  6.0 0.7 %copy-done.6 = f32[64]{0:T(128)S(1)} copy-done((f32[64]{0:T(128)S(1)}, f32[64]{0:T(128)}, u32[]{:S(2)}) %copy-start.6) | copy-done | bytes 280
  6.7 0.0 copy-start.7
  6.7 0.7 %copy-done.7 = s32[32]{0:T(128)S(1)} copy-done((s32[32]{0:T(128)S(1)}, s32[32]{0:T(128)}, u32[]{:S(2)}) %copy-start.7) | copy-done | bytes 152
  7.3 31.7 %shard_map.95 = (bf16[2,1,12,288,128]{4,3,2,1,0:T(8,128)(2,1)S(1)}, bf16[1,128,128]{2,1,0:T(8,128)(2,1)S(1)}, f32[1,8,128]{2,1,0:T(8,128)S(1)}) custom-call(bf16[12,12,24,128]{3,2,1,0:T(8,128)(2,1)S(1)} %bitcast.10, bf16[2,12,12,24,128]{4,3,2,1,0:T(8,128)(2,1)S(1)} %bitcast.9, f32[64]{0:T(128)S(1)} %copy-done.4, f32[64]{0:T(128)S(1)} %copy-done.6, ...), custom_call_target="tpu_custom_call" | custom-call | tf_op jit(solution)/shard_map/pallas_call | solution.py:419
  39.1 4.7 %shard_map.96 = (bf16[2,12,12,24,128]{4,3,2,1,0:T(8,128)(2,1)}, f32[8,32]{1,0:T(8,128)}) custom-call(f32[64]{0:T(128)S(1)} %copy-done.4, s32[64]{0:T(128)S(1)} %copy-done.5, bf16[2,1,12,288,128]{4,3,2,1,0:T(8,128)(2,1)S(1)} %get-tuple-element.7.shifted, bf16[1,128,128]{2,1,0:T(8,128)(2,1)S(1)} %get-tuple-element.8.mixing, ...), custom_call_target="tpu_custom_call" | custom-call | tf_op jit(solution)/shard_map/pallas_call | solution.py:457
Async XLA Ops:
  0.6 1.5 %copy-start = (bf16[2,2,12,12,12,128]{5,1,4,3,2,0:T(2,128)(2,1)S(1)}, bf16[2,2,12,12,12,128]{5,1,4,3,2,0:T(2,128)(2,1)}, u32[]{:S(2)}) copy-start(bf16[2,2,12,12,12,128]{5,1,4,3,2,0:T(2,128)(2,1)} %param.9) | copy-start | bytes 5308420
  2.1 1.2 %copy-start.1 = (bf16[2,12,12,12,128]{4,0,3,2,1:T(2,128)(2,1)S(1)}, bf16[2,12,12,12,128]{4,0,3,2,1:T(2,128)(2,1)}, u32[]{:S(2)}) copy-start(bf16[2,12,12,12,128]{4,0,3,2,1:T(2,128)(2,1)} %param.8) | copy-start | bytes 2654212
  3.3 0.7 %copy-start.2 = (s32[32,34]{1,0:T(8,128)S(1)}, s32[32,34]{1,0:T(8,128)}, u32[]{:S(2)}) copy-start(s32[32,34]{1,0:T(8,128)} %neighbours.1) | copy-start | bytes 13060
  4.0 0.7 %copy-start.3 = (bf16[32,34]{1,0:T(8,128)(2,1)S(1)}, bf16[32,34]{1,0:T(8,128)(2,1)}, u32[]{:S(2)}) copy-start(bf16[32,34]{1,0:T(8,128)(2,1)} %weight.1) | copy-start | bytes 6532
  4.7 0.7 %copy-start.4 = (f32[64]{0:T(128)S(1)}, f32[64]{0:T(128)}, u32[]{:S(2)}) copy-start(f32[64]{0:T(128)} %coupling.3) | copy-start | bytes 772
  5.3 0.7 %copy-start.5 = (s32[64]{0:T(128)S(1)}, s32[64]{0:T(128)}, u32[]{:S(2)}) copy-start(s32[64]{0:T(128)} %shifts.3) | copy-start | bytes 772
  6.0 0.7 %copy-start.6 = (f32[64]{0:T(128)S(1)}, f32[64]{0:T(128)}, u32[]{:S(2)}) copy-start(f32[64]{0:T(128)} %occupation.1) | copy-start | bytes 772
  6.7 0.7 %copy-start.7 = (s32[32]{0:T(128)S(1)}, s32[32]{0:T(128)}, u32[]{:S(2)}) copy-start(s32[32]{0:T(128)} %count.1) | copy-start | bytes 388

commit v2 on v1

--- a/solution.py
+++ b/solution.py
@@ -20,21 +20,33 @@
     return -(-value // step) * step
 
 
-def pieces(first, count):
-    parts, done = [], 0
-    while done < count:
-        tile, row = divmod(first + done, ROWS)
-        size = min(ROWS - row, count - done)
-        parts.append((tile, row, size, done))
-        done += size
+def row_plan(energies):
+    inner = energies - 2 * SHIFT
+    if inner <= 0:
+        return [(0, 0, energies), (1, 0, energies)], 2 * energies
+    ends = [(k, start, SHIFT) for k in range(2) for start in (0, energies - SHIFT)]
+    return ends + [(k, SHIFT, inner) for k in range(2)], 4 * SHIFT
+
+
+def pieces(energies):
+    parts, place = [], 0
+    for k, start, count in row_plan(energies)[0]:
+        done = 0
+        while done < count:
+            tile, row = divmod(place + done, ROWS)
+            size = min(ROWS - row, count - done)
+            parts.append((tile, row, size, k, start + done))
+            done += size
+        place += count
     return parts
 
 
 def keldysh_kernel(
     ne, nz, orb, energies, atoms, modes, slots,
-    green, broad, coupling, occupation, shifts, count, neighbours, weight,
-    shifted, mixing, summed,
+    green, broad, coupling_in, occupation_in, shifts_in, count_in, neighbours_in, weight_in,
+    shifted, mixing, share_out,
     gv, sv, plain, gf, sf, hf, ext, edge, send, recv, bonds, first, second,
+    coupling, occupation, shifts, count, neighbours, weight, small_sem,
     g_sem, s_sem, send_sem, recv_sem, bsend, brecv, fsend, frecv, ssend, srecv,
 ):
     e = lax.axis_index("energy")
@@ -42,6 +54,7 @@
     chunks = atoms // LANES
     pair_rows = 2 * energies
     tiles = pl.cdiv(pair_rows, ROWS)
+    edge_tiles = pl.cdiv(row_plan(energies)[1], ROWS)
     halo = 2 * SHIFT
     out_rows = ceil_to(pair_rows, ROWS)
     iblocks, jblocks = orb // IBLOCK, orb // JBLOCK
@@ -58,10 +71,25 @@
     def input_copies(lc):
         lanes = pl.ds(pl.multiple_of(lc * LANES, LANES), LANES)
         return (
-            pltpu.make_async_copy(green.at[:, :, :, lanes], gv, g_sem),
-            pltpu.make_async_copy(broad.at[:, :, :, :, lanes], sv, s_sem),
-        )
-
+            pltpu.make_async_copy(green.at[:, :, lanes], gv, g_sem),
+            pltpu.make_async_copy(broad.at[:, :, :, lanes], sv, s_sem),
+        )
+
+    small_copies = [
+        pltpu.make_async_copy(source, target, small_sem.at[index])
+        for index, (source, target) in enumerate(
+            (
+                (neighbours_in, neighbours),
+                (weight_in, weight),
+                (count_in, count),
+                (coupling_in, coupling),
+                (occupation_in, occupation),
+                (shifts_in, shifts),
+            )
+        )
+    ]
+    for copy in small_copies:
+        copy.start()
     if chunks == 1:
         for copy in input_copies(0):
             copy.start()
@@ -79,6 +107,9 @@
     def _(step):
         target = {"energy": lax.rem(e + step, ne), "atom": z}
         pl.semaphore_signal(barrier, inc=1, device_id=target, device_id_type=MESH)
+
+    for copy in small_copies:
+        copy.wait()
 
     row_id = lax.broadcasted_iota(jnp.int32, (tile_width, slots), 0)
     slot_id = lax.broadcasted_iota(jnp.int32, (tile_width, slots), 1)
@@ -141,6 +172,12 @@
             for form in range(count_of):
                 target[tile, form, index, :, 0:size] = forms[form]
 
+    def spread(blocks):
+        begin = 0
+        for k, start, size in row_plan(energies)[0]:
+            plain[:, begin : begin + 2 * size] = blocks[k][:, 2 * start : 2 * (start + size)]
+            begin += 2 * size
+
     def prepare(lc):
         g_copy, s_copy = input_copies(lc)
         if chunks > 1:
@@ -150,30 +187,29 @@
 
         @pl.loop(0, orb)
         def _(i):
-            block = gv[i].astype(jnp.float32)
-            plain[:, 0:pair_rows] = block
-            plain[:, pair_rows : 2 * pair_rows] = block
+            block = gv[i].astype(jnp.float32).reshape(orb, pair_rows, LANES)
+            spread((block, block))
             store_forms(gf, i, 4)
 
         s_copy.wait()
 
         @pl.loop(0, orb)
         def _(i):
-            for k in range(2):
-                plain[:, k * pair_rows : (k + 1) * pair_rows] = sv[k, i].astype(jnp.float32)
+            spread(
+                [sv[k, i].astype(jnp.float32).reshape(orb, pair_rows, LANES) for k in range(2)]
+            )
             store_forms(sf, i, 3)
 
     def keldysh_chunk(lc):
         if chunks > 1:
             prepare(lc)
 
-        @pl.loop(0, iblocks)
-        def _(ib):
+        def products(ib, first_tile, last_tile):
             irows = pl.ds(ib * IBLOCK, IBLOCK)
 
-            @pl.loop(0, tiles * jblocks)
+            @pl.loop(0, (last_tile - first_tile) * jblocks)
             def _(step):
-                tile, jb = step // jblocks, lax.rem(step, jblocks)
+                tile, jb = first_tile + step // jblocks, lax.rem(step, jblocks)
                 jrows = pl.ds(jb * JBLOCK, JBLOCK)
                 total = [None] * 3
                 for inner in range(orb):
@@ -188,7 +224,7 @@
             @pl.loop(0, jblocks)
             def _(jb):
                 jrows = pl.ds(jb * JBLOCK, JBLOCK)
-                for tile in range(tiles):
+                for tile in range(first_tile, last_tile):
                     total = [None] * 3
                     for inner in range(orb):
                         for form, other in enumerate((0, 1, 3)):
@@ -196,14 +232,17 @@
                             total[form] = term if inner == 0 else total[form] + term
                     parts = (total[0] + total[1], total[2] - total[0] + total[1])
                     for c, value in enumerate(parts):
-                        for k in range(2):
-                            for t, row, size, done in pieces(k * energies, energies):
-                                if t == tile:
-                                    start = halo + 2 * done + c
-                                    ext[lc, k, irows, jrows, pl.ds(start, size, stride=2)] = value[
-                                        :, :, row : row + size
-                                    ]
-
+                        for t, row, size, k, energy in pieces(energies):
+                            if t == tile:
+                                start = halo + 2 * energy + c
+                                ext[lc, k, irows, jrows, pl.ds(start, size, stride=2)] = value[
+                                    :, :, row : row + size
+                                ]
+
+        @pl.loop(0, iblocks)
+        def _(ib):
+            irows = pl.ds(ib * IBLOCK, IBLOCK)
+            products(ib, 0, edge_tiles)
             for side, start in enumerate((halo, pair_rows)):
                 for k in range(2):
                     for j in range(orb):
@@ -213,6 +252,11 @@
                         ]
                 send[lc, side, ib] = edge[side].astype(jnp.bfloat16)
                 halo_copy(lc, ib, side).start()
+
+        if edge_tiles < tiles:
+            @pl.loop(0, iblocks)
+            def _(ib):
+                products(ib, edge_tiles, tiles)
 
     if chunks == 1:
         prepare(0)
@@ -361,41 +405,39 @@
     def _(step):
         second_copy(step).wait()
 
-    summed[...] = jnp.sum(second[...], axis=0)
-
-
-def mixing_kernel(ne, nz, orb, energies, atoms, modes, coupling, shifts, shifted, mixing, summed, out, pol):
+    summed = jnp.sum(second[...], axis=0)
+    own = jnp.zeros((ROWS, tile_width), jnp.float32)
+    for tile in range(nz):
+        lc, lane = divmod(tile * tile_width, LANES)
+        own = jnp.where(z == tile, summed[lc, :, lane : lane + tile_width], own)
+    share = modes // ne
+    scale = 1.0 / math.sqrt(energies * ne * nz)
+    for row in range(share):
+        mode = e * share + row
+        shift = shifts[mode]
+        line = jnp.zeros((1, tile_width), jnp.float32)
+        for level in range(1, SHIFT + 1):
+            line += jnp.where(shift == level, 1.0, 0.0) * own[level - 1 : level]
+        share_out[row : row + 1] = line * (coupling[mode] * scale)
+
+
+def mixing_kernel(orb, energies, atoms, shifted, mixing, share, out, pol):
     chunks = atoms // LANES
     pair_rows = 2 * energies
     out_rows = ceil_to(pair_rows, ROWS)
-    for row in range(IBLOCK):
+    for row in range(out.shape[1]):
         mixed = None
         for lc in range(chunks):
             product = jnp.dot(
                 shifted[0, lc, row], mixing[lc], preferred_element_type=jnp.float32
             )
             mixed = product if mixed is None else mixed + product
-        mixed = mixed.reshape(orb, out_rows, atoms)
-        out[0, row] = mixed[:, :pair_rows].astype(jnp.bfloat16)
-
-    @pl.when((pl.program_id(0) == 0) & (pl.program_id(1) == 0))
-    def _():
-        e = lax.axis_index("energy")
-        z = lax.axis_index("atom")
-        tile_width = atoms // nz
-        own = jnp.zeros((ROWS, tile_width), jnp.float32)
-        for tile in range(nz):
-            lc, lane = divmod(tile * tile_width, LANES)
-            own = jnp.where(z == tile, summed[lc, :, lane : lane + tile_width], own)
-        share = modes // ne
-        scale = 1.0 / math.sqrt(energies * ne * nz)
-        for row in range(share):
-            mode = e * share + row
-            shift = shifts[mode]
-            line = jnp.zeros((1, tile_width), jnp.float32)
-            for level in range(1, SHIFT + 1):
-                line += jnp.where(shift == level, 1.0, 0.0) * own[level - 1 : level]
-            pol[row : row + 1] = line * (coupling[mode] * scale)
+        if out_rows != pair_rows:
+            mixed = mixed.reshape(orb, out_rows, atoms)[:, :pair_rows]
+            mixed = mixed.reshape(orb * pair_rows, atoms)
+        out[0, row] = mixed.astype(jnp.bfloat16)
+
+    pol[...] = share[...]
 
 
 def local(ne, nz, green_ret, broadening, coupling, occupation, shifts, neighbours, bond_count, bond_weight):
@@ -412,22 +454,21 @@
     halo_shape = (chunks, 2, iblocks) + edge_shape
     dma = pltpu.SemaphoreType.DMA
     vmem = pl.BlockSpec(memory_space=pltpu.VMEM)
-    smem = pl.BlockSpec(memory_space=pltpu.SMEM)
-    anywhere = pl.BlockSpec(memory_space=pl.ANY)
-    green = green_ret.transpose(1, 2, 3, 0, 4).reshape(orb, orb, pair_rows, atoms)
-    broad = broadening.transpose(0, 2, 3, 4, 1, 5).reshape(2, orb, orb, pair_rows, atoms)
-    shifted, mixing, summed = pl.pallas_call(
+    hbm = pl.BlockSpec(memory_space=pltpu.HBM)
+    green = green_ret.transpose(1, 2, 3, 0, 4).reshape(orb, orb * pair_rows, atoms)
+    broad = broadening.transpose(0, 2, 3, 4, 1, 5).reshape(2, orb, orb * pair_rows, atoms)
+    shifted, mixing, share = pl.pallas_call(
         functools.partial(keldysh_kernel, ne, nz, orb, energies, atoms, modes, slots),
         out_shape=(
             jax.ShapeDtypeStruct((2, chunks, orb, orb * out_rows, LANES), jnp.bfloat16),
             jax.ShapeDtypeStruct((chunks, LANES, atoms), jnp.bfloat16),
-            jax.ShapeDtypeStruct((chunks, ROWS, LANES), jnp.float32),
+            jax.ShapeDtypeStruct((modes // ne, tile_width), jnp.float32),
         ),
-        in_specs=[anywhere, anywhere, smem, smem, smem, smem, vmem, vmem],
+        in_specs=[hbm] * 8,
         out_specs=(vmem, vmem, vmem),
         scratch_shapes=[
-            pltpu.VMEM((orb, orb, pair_rows, LANES), jnp.bfloat16),
-            pltpu.VMEM((2, orb, orb, pair_rows, LANES), jnp.bfloat16),
+            pltpu.VMEM((orb, orb * pair_rows, LANES), jnp.bfloat16),
+            pltpu.VMEM((2, orb, orb * pair_rows, LANES), jnp.bfloat16),
             pltpu.VMEM((orb, 2 * pair_rows, LANES), jnp.float32),
             pltpu.VMEM((tiles, 4, orb, orb, ROWS, LANES), jnp.float32),
             pltpu.VMEM((tiles, 3, orb, orb, ROWS, LANES), jnp.float32),
@@ -439,6 +480,13 @@
             pltpu.VMEM((nz, tile_width, atoms), jnp.bfloat16),
             pltpu.VMEM((nz, chunks, ROWS, LANES), jnp.float32),
             pltpu.VMEM((ne, chunks, ROWS, LANES), jnp.float32),
+            pltpu.SMEM((modes,), jnp.float32),
+            pltpu.SMEM((modes,), jnp.float32),
+            pltpu.SMEM((modes,), jnp.int32),
+            pltpu.SMEM((tile_width,), jnp.int32),
+            pltpu.VMEM(neighbours.shape, jnp.int32),
+            pltpu.VMEM(bond_weight.shape, jnp.bfloat16),
+            dma((6,)),
             dma,
             dma,
             dma((chunks, 2, iblocks)),
@@ -451,29 +499,27 @@
             dma((ne,)),
         ],
         compiler_params=pltpu.CompilerParams(
-            collective_id=0, has_side_effects=True, vmem_limit_bytes=48 * 1024 * 1024
+            collective_id=0, has_side_effects=True, vmem_limit_bytes=64 * 1024 * 1024
         ),
     )(green, broad, coupling, occupation, shifts, bond_count, neighbours, bond_weight)
     out, pol = pl.pallas_call(
-        functools.partial(mixing_kernel, ne, nz, orb, energies, atoms, modes),
-        grid=(2, iblocks),
+        functools.partial(mixing_kernel, orb, energies, atoms),
+        grid=(2, 2),
         out_shape=(
-            jax.ShapeDtypeStruct((2, orb, orb, pair_rows, atoms), jnp.bfloat16),
+            jax.ShapeDtypeStruct((2, orb, orb * pair_rows, atoms), jnp.bfloat16),
             jax.ShapeDtypeStruct((modes // ne, tile_width), jnp.float32),
         ),
         in_specs=[
-            smem,
-            smem,
-            pl.BlockSpec((1, chunks, IBLOCK, orb * out_rows, LANES), lambda k, ib: (k, 0, ib, 0, 0)),
+            pl.BlockSpec((1, chunks, orb // 2, orb * out_rows, LANES), lambda k, ib: (k, 0, ib, 0, 0)),
             pl.BlockSpec((chunks, LANES, atoms), lambda k, ib: (0, 0, 0)),
-            pl.BlockSpec((chunks, ROWS, LANES), lambda k, ib: (0, 0, 0)),
+            pl.BlockSpec((modes // ne, tile_width), lambda k, ib: (0, 0)),
         ],
         out_specs=(
-            pl.BlockSpec((1, IBLOCK, orb, pair_rows, atoms), lambda k, ib: (k, ib, 0, 0, 0)),
+            pl.BlockSpec((1, orb // 2, orb * pair_rows, atoms), lambda k, ib: (k, ib, 0, 0)),
             pl.BlockSpec((modes // ne, tile_width), lambda k, ib: (0, 0)),
         ),
-        compiler_params=pltpu.CompilerParams(vmem_limit_bytes=24 * 1024 * 1024),
-    )(coupling, shifts, shifted, mixing, summed)
+        compiler_params=pltpu.CompilerParams(vmem_limit_bytes=64 * 1024 * 1024),
+    )(shifted, mixing, share)
     self_energy = out.reshape(2, orb, orb, energies, 2, atoms).transpose(0, 4, 1, 2, 3, 5)
     return self_energy, pol
 

time: 44.1 us -> 36 us (0.82)
  local copies, waits for them, and re-layouts: 6.67 us -> 0 us
  Pallas kernels: 36.5 us -> 35.1 us
    unnamed x16 -> x0, local copies, waits for them, and re-layouts: 6.67 us -> none
    pallas_call x1, Pallas kernels: 31.7 us -> 31 us  [local(): pl.pallas_call(functools.partial(keldysh_kernel, ne, nz, orb, energies, a...]
    pallas_call x1, Pallas kernels: 4.71 us -> 4.13 us  [local(): pl.pallas_call(functools.partial(mixing_kernel, orb, energies, atoms), gr...]
where the time goes in v2:
time: 36 us; the launch traced here: 35.8 us
  Pallas kernels  35.1 us (98%)
  between operations  0.64 us (2%)
    pallas_call x1, Pallas kernels, local(): pl.pallas_call(functools.partial(keldysh_kernel, ne, nz, orb, energies, a...  31 us
    pallas_call x1, Pallas kernels, local(): pl.pallas_call(functools.partial(mixing_kernel, orb, energies, atoms), gr...  4.13 us

profile of v2, /device:TPU:0, one launch (start us, length us, event | category | flops | bytes accessed | tf_op | source)
XLA Modules:
  0.0 35.8 jit_solution(9359744815417792018)
XLA Ops:
  0.6 31.0 %shard_map.95 = (bf16[2,1,12,288,128]{4,3,2,1,0:T(8,128)(2,1)}, bf16[1,128,128]{2,1,0:T(8,128)(2,1)}, f32[8,32]{1,0:T(8,128)}) custom-call(bf16[12,288,128]{2,1,0:T(8,128)(2,1)} %bitcast.10, bf16[2,12,288,128]{3,2,1,0:T(8,128)(2,1)} %bitcast.9, f32[64]{0:T(128)} %coupling_in.1, f32[64]{0:T(128)} %occupation_in.1, s32[64]{0:T(128)} %shifts_in.1, s32[32]{0:T(128)} %count_in.1, ...), custom_call_target="tpu_custom_call" | custom-call | tf_op jit(solution)/shard_map/pallas_call | solution.py:460
  31.7 4.1 %shard_map.96 = (bf16[2,12,288,128]{3,2,1,0:T(8,128)(2,1)}, f32[8,32]{1,0:T(8,128)}) custom-call(bf16[2,1,12,288,128]{4,3,2,1,0:T(8,128)(2,1)} %get-tuple-element.7.shifted, bf16[1,128,128]{2,1,0:T(8,128)(2,1)} %get-tuple-element.8.mixing, f32[8,32]{1,0:T(8,128)} %get-tuple-element.9.share), custom_call_target="tpu_custom_call" | custom-call | tf_op jit(solution)/shard_map/pallas_call | solution.py:505

commit v3 on v2

--- a/solution.py
+++ b/solution.py
@@ -26,6 +26,13 @@
         return [(0, 0, energies), (1, 0, energies)], 2 * energies
     ends = [(k, start, SHIFT) for k in range(2) for start in (0, energies - SHIFT)]
     return ends + [(k, SHIFT, inner) for k in range(2)], 4 * SHIFT
+
+
+def green_tiles(energies):
+    edges, inner = row_plan(energies)[1], energies - 2 * SHIFT
+    if inner > 0 and edges % ROWS == 0 and inner % ROWS == 0:
+        return edges // ROWS + inner // ROWS
+    return pl.cdiv(2 * energies, ROWS)
 
 
 def pieces(energies):
@@ -44,9 +51,9 @@
 def keldysh_kernel(
     ne, nz, orb, energies, atoms, modes, slots,
     green, broad, coupling_in, occupation_in, shifts_in, count_in, neighbours_in, weight_in,
-    shifted, mixing, share_out,
-    gv, sv, plain, gf, sf, hf, ext, edge, send, recv, bonds, first, second,
-    coupling, occupation, shifts, count, neighbours, weight, small_sem,
+    out, share_out,
+    gv, sv, plain, gf, sf, hf, ext, edge, send, recv, bonds, mixing, result, first, second,
+    mode_rows, mode_shifts, coupling, shifts, count, neighbours, weight, small_sem, out_sem,
     g_sem, s_sem, send_sem, recv_sem, bsend, brecv, fsend, frecv, ssend, srecv,
 ):
     e = lax.axis_index("energy")
@@ -55,6 +62,7 @@
     pair_rows = 2 * energies
     tiles = pl.cdiv(pair_rows, ROWS)
     edge_tiles = pl.cdiv(row_plan(energies)[1], ROWS)
+    repeat = green_tiles(energies)
     halo = 2 * SHIFT
     out_rows = ceil_to(pair_rows, ROWS)
     iblocks, jblocks = orb // IBLOCK, orb // JBLOCK
@@ -83,8 +91,10 @@
                 (weight_in, weight),
                 (count_in, count),
                 (coupling_in, coupling),
-                (occupation_in, occupation),
                 (shifts_in, shifts),
+                (coupling_in, mode_rows.at[0]),
+                (occupation_in, mode_rows.at[1]),
+                (shifts_in, mode_shifts),
             )
         )
     ]
@@ -126,20 +136,13 @@
         )
     bonds[z] = bond_rows.astype(jnp.bfloat16)
 
-    def add_mode(q, sums):
-        strength, filling, shift = coupling[q], occupation[q], shifts[q]
-        emit, absorb = strength * (filling + 1.0), strength * filling
-        return tuple(
-            total + jnp.where(shift == level, term, 0.0)
-            for level, pair in enumerate(zip(sums[::2], sums[1::2]), 1)
-            for total, term in zip(pair, (emit, absorb))
-        )
-
-    sums = lax.fori_loop(0, modes, add_mode, (jnp.float32(0.0),) * (2 * SHIFT))
-    rounded = [
-        jnp.full((out_rows, LANES), total, jnp.float32).astype(jnp.bfloat16).astype(jnp.float32)
-        for total in sums
-    ]
+    strength, filling, level_of = mode_rows[0], mode_rows[1], mode_shifts[...]
+    rounded = []
+    for level in range(1, SHIFT + 1):
+        for factor in (strength * (filling + 1.0), strength * filling):
+            total = jnp.sum(jnp.where(level_of == level, factor, 0.0), axis=1, keepdims=True)
+            total = total.astype(jnp.bfloat16).astype(jnp.float32)
+            rounded.append(jnp.broadcast_to(total, (out_rows, LANES)))
     emission, absorption = rounded[::2], rounded[1::2]
 
     def bond_copy(step):
@@ -162,8 +165,11 @@
             device_id_type=MESH,
         )
 
+    def green_tile(tile):
+        return jnp.where(tile >= repeat, tile - (repeat - edge_tiles), tile)
+
     def store_forms(target, index, count_of):
-        for tile in range(tiles):
+        for tile in range(target.shape[0]):
             low = tile * ROWS
             size = min(ROWS, pair_rows - low)
             real = plain[:, pl.ds(2 * low, size, stride=2)]
@@ -172,10 +178,11 @@
             for form in range(count_of):
                 target[tile, form, index, :, 0:size] = forms[form]
 
-    def spread(blocks):
+    def spread(blocks, limit):
         begin = 0
         for k, start, size in row_plan(energies)[0]:
-            plain[:, begin : begin + 2 * size] = blocks[k][:, 2 * start : 2 * (start + size)]
+            if begin < 2 * limit:
+                plain[:, begin : begin + 2 * size] = blocks[k][:, 2 * start : 2 * (start + size)]
             begin += 2 * size
 
     def prepare(lc):
@@ -188,7 +195,7 @@
         @pl.loop(0, orb)
         def _(i):
             block = gv[i].astype(jnp.float32).reshape(orb, pair_rows, LANES)
-            spread((block, block))
+            spread((block, block), repeat * ROWS)
             store_forms(gf, i, 4)
 
         s_copy.wait()
@@ -196,7 +203,8 @@
         @pl.loop(0, orb)
         def _(i):
             spread(
-                [sv[k, i].astype(jnp.float32).reshape(orb, pair_rows, LANES) for k in range(2)]
+                [sv[k, i].astype(jnp.float32).reshape(orb, pair_rows, LANES) for k in range(2)],
+                pair_rows,
             )
             store_forms(sf, i, 3)
 
@@ -211,10 +219,11 @@
             def _(step):
                 tile, jb = first_tile + step // jblocks, lax.rem(step, jblocks)
                 jrows = pl.ds(jb * JBLOCK, JBLOCK)
+                source = green_tile(tile)
                 total = [None] * 3
                 for inner in range(orb):
                     for form in range(3):
-                        term = gf[tile, form, irows, inner][:, None] * sf[tile, form, inner, jrows][None]
+                        term = gf[source, form, irows, inner][:, None] * sf[tile, form, inner, jrows][None]
                         total[form] = term if inner == 0 else total[form] + term
                 real = total[0] - total[1]
                 imag = total[2] - total[0] - total[1]
@@ -225,10 +234,11 @@
             def _(jb):
                 jrows = pl.ds(jb * JBLOCK, JBLOCK)
                 for tile in range(first_tile, last_tile):
+                    source = tile if tile < repeat else tile - (repeat - edge_tiles)
                     total = [None] * 3
                     for inner in range(orb):
                         for form, other in enumerate((0, 1, 3)):
-                            term = hf[tile, form, :, inner][:, None] * gf[tile, other, jrows, inner][None]
+                            term = hf[tile, form, :, inner][:, None] * gf[source, other, jrows, inner][None]
                             total[form] = term if inner == 0 else total[form] + term
                     parts = (total[0] + total[1], total[2] - total[0] + total[1])
                     for c, value in enumerate(parts):
@@ -371,23 +381,33 @@
     def shift_energies(k):
         upward, downward = (emission, absorption) if k == 0 else (absorption, emission)
 
-        @pl.loop(0, chunks * orb)
-        def _(step):
-            lc, i = step // orb, lax.rem(step, orb)
-            total = None
-            for offset in range(1, SHIFT + 1):
-                for sign, factor in ((1, upward[offset - 1]), (-1, downward[offset - 1])):
-                    start = halo + 2 * sign * offset
-                    term = factor[None] * ext[lc, k, i, :, start : start + out_rows]
-                    total = term if total is None else total + term
-            flat = total.reshape(orb * out_rows, LANES)
-            shifted[k, lc, i] = flat.astype(jnp.bfloat16)
+        @pl.loop(0, orb)
+        def _(i):
+            mixed = None
+            for lc in range(chunks):
+                total = None
+                for offset in range(1, SHIFT + 1):
+                    for sign, factor in ((1, upward[offset - 1]), (-1, downward[offset - 1])):
+                        start = halo + 2 * sign * offset
+                        term = factor[None] * ext[lc, k, i, :, start : start + out_rows]
+                        total = term if total is None else total + term
+                flat = total.reshape(orb * out_rows, LANES).astype(jnp.bfloat16)
+                product = jnp.dot(flat, mixing[lc], preferred_element_type=jnp.float32)
+                mixed = product if mixed is None else mixed + product
+            if out_rows != pair_rows:
+                mixed = mixed.reshape(orb, out_rows, atoms)[:, :pair_rows]
+                mixed = mixed.reshape(orb * pair_rows, atoms)
+            result[k, i] = mixed.astype(jnp.bfloat16)
+
+    def out_copy(k):
+        return pltpu.make_async_copy(result.at[k], out.at[k], out_sem.at[k])
 
     @pl.loop(1, nz)
     def _(step):
         first_copy(step).start()
 
     shift_energies(0)
+    out_copy(0).start()
 
     @pl.loop(1, nz)
     def _(step):
@@ -400,6 +420,7 @@
         second_copy(step).start()
 
     shift_energies(1)
+    out_copy(1).start()
 
     @pl.loop(1, ne)
     def _(step):
@@ -414,30 +435,13 @@
     scale = 1.0 / math.sqrt(energies * ne * nz)
     for row in range(share):
         mode = e * share + row
-        shift = shifts[mode]
+        shift = shifts[0, mode]
         line = jnp.zeros((1, tile_width), jnp.float32)
         for level in range(1, SHIFT + 1):
             line += jnp.where(shift == level, 1.0, 0.0) * own[level - 1 : level]
-        share_out[row : row + 1] = line * (coupling[mode] * scale)
-
-
-def mixing_kernel(orb, energies, atoms, shifted, mixing, share, out, pol):
-    chunks = atoms // LANES
-    pair_rows = 2 * energies
-    out_rows = ceil_to(pair_rows, ROWS)
-    for row in range(out.shape[1]):
-        mixed = None
-        for lc in range(chunks):
-            product = jnp.dot(
-                shifted[0, lc, row], mixing[lc], preferred_element_type=jnp.float32
-            )
-            mixed = product if mixed is None else mixed + product
-        if out_rows != pair_rows:
-            mixed = mixed.reshape(orb, out_rows, atoms)[:, :pair_rows]
-            mixed = mixed.reshape(orb * pair_rows, atoms)
-        out[0, row] = mixed.astype(jnp.bfloat16)
-
-    pol[...] = share[...]
+        share_out[row : row + 1] = line * (coupling[0, mode] * scale)
+    for k in range(2):
+        out_copy(k).wait()
 
 
 def local(ne, nz, green_ret, broadening, coupling, occupation, shifts, neighbours, bond_count, bond_weight):
@@ -457,20 +461,19 @@
     hbm = pl.BlockSpec(memory_space=pltpu.HBM)
     green = green_ret.transpose(1, 2, 3, 0, 4).reshape(orb, orb * pair_rows, atoms)
     broad = broadening.transpose(0, 2, 3, 4, 1, 5).reshape(2, orb, orb * pair_rows, atoms)
-    shifted, mixing, share = pl.pallas_call(
+    out, pol = pl.pallas_call(
         functools.partial(keldysh_kernel, ne, nz, orb, energies, atoms, modes, slots),
         out_shape=(
-            jax.ShapeDtypeStruct((2, chunks, orb, orb * out_rows, LANES), jnp.bfloat16),
-            jax.ShapeDtypeStruct((chunks, LANES, atoms), jnp.bfloat16),
+            jax.ShapeDtypeStruct((2, orb, orb * pair_rows, atoms), jnp.bfloat16),
             jax.ShapeDtypeStruct((modes // ne, tile_width), jnp.float32),
         ),
         in_specs=[hbm] * 8,
-        out_specs=(vmem, vmem, vmem),
+        out_specs=(hbm, vmem),
         scratch_shapes=[
             pltpu.VMEM((orb, orb * pair_rows, LANES), jnp.bfloat16),
             pltpu.VMEM((2, orb, orb * pair_rows, LANES), jnp.bfloat16),
             pltpu.VMEM((orb, 2 * pair_rows, LANES), jnp.float32),
-            pltpu.VMEM((tiles, 4, orb, orb, ROWS, LANES), jnp.float32),
+            pltpu.VMEM((green_tiles(energies), 4, orb, orb, ROWS, LANES), jnp.float32),
             pltpu.VMEM((tiles, 3, orb, orb, ROWS, LANES), jnp.float32),
             pltpu.VMEM((tiles, 3, IBLOCK, orb, ROWS, LANES), jnp.float32),
             pltpu.VMEM((chunks, 2, orb, orb, ext_rows, LANES), jnp.float32),
@@ -478,15 +481,19 @@
             pltpu.VMEM(halo_shape, jnp.bfloat16),
             pltpu.VMEM(halo_shape, jnp.bfloat16),
             pltpu.VMEM((nz, tile_width, atoms), jnp.bfloat16),
+            pltpu.VMEM((chunks, LANES, atoms), jnp.bfloat16),
+            pltpu.VMEM((2, orb, orb * pair_rows, atoms), jnp.bfloat16),
             pltpu.VMEM((nz, chunks, ROWS, LANES), jnp.float32),
             pltpu.VMEM((ne, chunks, ROWS, LANES), jnp.float32),
-            pltpu.SMEM((modes,), jnp.float32),
-            pltpu.SMEM((modes,), jnp.float32),
-            pltpu.SMEM((modes,), jnp.int32),
+            pltpu.VMEM((2, 1, modes), jnp.float32),
+            pltpu.VMEM((1, modes), jnp.int32),
+            pltpu.SMEM((1, modes), jnp.float32),
+            pltpu.SMEM((1, modes), jnp.int32),
             pltpu.SMEM((tile_width,), jnp.int32),
             pltpu.VMEM(neighbours.shape, jnp.int32),
             pltpu.VMEM(bond_weight.shape, jnp.bfloat16),
-            dma((6,)),
+            dma((8,)),
+            dma((2,)),
             dma,
             dma,
             dma((chunks, 2, iblocks)),
@@ -501,25 +508,16 @@
         compiler_params=pltpu.CompilerParams(
             collective_id=0, has_side_effects=True, vmem_limit_bytes=64 * 1024 * 1024
         ),
-    )(green, broad, coupling, occupation, shifts, bond_count, neighbours, bond_weight)
-    out, pol = pl.pallas_call(
-        functools.partial(mixing_kernel, orb, energies, atoms),
-        grid=(2, 2),
-        out_shape=(
-            jax.ShapeDtypeStruct((2, orb, orb * pair_rows, atoms), jnp.bfloat16),
-            jax.ShapeDtypeStruct((modes // ne, tile_width), jnp.float32),
-        ),
-        in_specs=[
-            pl.BlockSpec((1, chunks, orb // 2, orb * out_rows, LANES), lambda k, ib: (k, 0, ib, 0, 0)),
-            pl.BlockSpec((chunks, LANES, atoms), lambda k, ib: (0, 0, 0)),
-            pl.BlockSpec((modes // ne, tile_width), lambda k, ib: (0, 0)),
-        ],
-        out_specs=(
-            pl.BlockSpec((1, orb // 2, orb * pair_rows, atoms), lambda k, ib: (k, ib, 0, 0)),
-            pl.BlockSpec((modes // ne, tile_width), lambda k, ib: (0, 0)),
-        ),
-        compiler_params=pltpu.CompilerParams(vmem_limit_bytes=64 * 1024 * 1024),
-    )(shifted, mixing, share)
+    )(
+        green,
+        broad,
+        coupling.reshape(1, modes),
+        occupation.reshape(1, modes),
+        shifts.reshape(1, modes),
+        bond_count,
+        neighbours,
+        bond_weight,
+    )
     self_energy = out.reshape(2, orb, orb, energies, 2, atoms).transpose(0, 4, 1, 2, 3, 5)
     return self_energy, pol
 

time: 36 us -> 35.3 us (0.981)
  Pallas kernels: 35.1 us -> 29.9 us
  local copies, waits for them, and re-layouts: 0 us -> 4.49 us
    unnamed x0 -> x4, local copies, waits for them, and re-layouts: none -> 4.49 us
    pallas_call x1 -> x0, Pallas kernels: 4.13 us -> none  [local(): pl.pallas_call(functools.partial(mixing_kernel, orb, energies, atoms), gr...]
    pallas_call x1, Pallas kernels: 31 us -> 29.9 us  [local(): pl.pallas_call(functools.partial(keldysh_kernel, ne, nz, orb, energies, a...]
where the time goes in v3:
time: 35.3 us; the launch traced here: 35 us
  Pallas kernels  29.9 us (85%)
  local copies, waits for them, and re-layouts  4.49 us (13%)
  between operations  0.65 us (2%)
    pallas_call x1, Pallas kernels, local(): pl.pallas_call(functools.partial(keldysh_kernel, ne, nz, orb, energies, a...  29.9 us
    unnamed x4, local copies, waits for them, and re-layouts  4.49 us

profile of v3, /device:TPU:0, one launch (start us, length us, event | category | flops | bytes accessed | tf_op | source)
XLA Modules:
  0.0 35.0 jit_solution(8736686510611683271)
XLA Ops:
  0.6 29.9 %shard_map.95 = (bf16[2,12,288,128]{3,2,1,0:T(8,128)(2,1)}, f32[8,32]{1,0:T(8,128)}) custom-call(bf16[12,288,128]{2,1,0:T(8,128)(2,1)} %bitcast.14, bf16[2,12,288,128]{3,2,1,0:T(8,128)(2,1)} %bitcast.13, f32[1,64]{1,0:T(1,128)} %bitcast.15, f32[1,64]{1,0:T(1,128)} %bitcast.16, s32[1,64]{1,0:T(1,128)} %bitcast.17, s32[32]{0:T(128)} %count_in.1, ...), custom_call_target="tpu_custom_call" | custom-call | tf_op jit(solution)/shard_map/pallas_call | solution.py:464
  30.5 0.0 copy-start
  30.5 3.9 %copy.12 = bf16[2,2,12,12,12,128]{5,1,4,3,2,0:T(2,128)(2,1)} copy(bf16[2,2,12,12,12,128]{5,1,4,3,2,0:T(2,128)(2,1)} %bitcast.12) | data formatting | bytes 3538944
  34.4 0.0 copy-done
  34.4 0.6 %copy.13 = f32[8,32]{1,0:T(8,128)} copy(f32[8,32]{1,0:T(8,128)S(1)} %copy-done) | data formatting | bytes 2048
Async XLA Ops:
  30.5 3.9 %copy-start = (f32[8,32]{1,0:T(8,128)S(1)}, f32[8,32]{1,0:T(8,128)}, u32[]{:S(2)}) copy-start(f32[8,32]{1,0:T(8,128)} %get-tuple-element.9) | copy-start | bytes 3076

commit v4 on v3

--- a/solution.py
+++ b/solution.py
@@ -11,8 +11,9 @@
 SHIFT = 2
 LANES = 128
 ROWS = 8
-IBLOCK = 3
-JBLOCK = 4
+IBLOCK = 6
+JBLOCK = 6
+PACK = 4
 MESH = pl.DeviceIdType.MESH
 
 
@@ -52,7 +53,7 @@
     ne, nz, orb, energies, atoms, modes, slots,
     green, broad, coupling_in, occupation_in, shifts_in, count_in, neighbours_in, weight_in,
     out, share_out,
-    gv, sv, plain, gf, sf, hf, ext, edge, send, recv, bonds, mixing, result, first, second,
+    gv, sv, plain, gf, sf, part, hf, ext, edge, send, recv, bonds, mixing, result, first, second,
     mode_rows, mode_shifts, coupling, shifts, count, neighbours, weight, small_sem, out_sem,
     g_sem, s_sem, send_sem, recv_sem, bsend, brecv, fsend, frecv, ssend, srecv,
 ):
@@ -215,32 +216,46 @@
         def products(ib, first_tile, last_tile):
             irows = pl.ds(ib * IBLOCK, IBLOCK)
 
+            def block_products(pick):
+                for form in range(3):
+                    total = None
+                    for inner in range(orb):
+                        one, two = pick(form, inner)
+                        term = one[:, None] * two[None]
+                        total = term if inner == 0 else total + term
+                    part[form] = total
+
             @pl.loop(0, (last_tile - first_tile) * jblocks)
             def _(step):
                 tile, jb = first_tile + step // jblocks, lax.rem(step, jblocks)
                 jrows = pl.ds(jb * JBLOCK, JBLOCK)
                 source = green_tile(tile)
-                total = [None] * 3
-                for inner in range(orb):
-                    for form in range(3):
-                        term = gf[source, form, irows, inner][:, None] * sf[tile, form, inner, jrows][None]
-                        total[form] = term if inner == 0 else total[form] + term
-                real = total[0] - total[1]
-                imag = total[2] - total[0] - total[1]
-                for form, value in enumerate((real, imag, real + imag)):
-                    hf[tile, form, :, jrows] = value
+                block_products(
+                    lambda form, inner: (
+                        gf[source, form, irows, inner],
+                        sf[tile, form, inner, jrows],
+                    )
+                )
+                for i in range(IBLOCK):
+                    one, two, mixed = part[0, i], part[1, i], part[2, i]
+                    real = one - two
+                    imag = mixed - one - two
+                    for form, value in enumerate((real, imag, real + imag)):
+                        hf[tile, form, i, jrows] = value
 
             @pl.loop(0, jblocks)
             def _(jb):
                 jrows = pl.ds(jb * JBLOCK, JBLOCK)
                 for tile in range(first_tile, last_tile):
                     source = tile if tile < repeat else tile - (repeat - edge_tiles)
-                    total = [None] * 3
-                    for inner in range(orb):
-                        for form, other in enumerate((0, 1, 3)):
-                            term = hf[tile, form, :, inner][:, None] * gf[source, other, jrows, inner][None]
-                            total[form] = term if inner == 0 else total[form] + term
-                    parts = (total[0] + total[1], total[2] - total[0] + total[1])
+                    block_products(
+                        lambda form, inner: (
+                            hf[tile, form, :, inner],
+                            gf[source, (0, 1, 3)[form], jrows, inner],
+                        )
+                    )
+                    one, two, mixed = part[0], part[1], part[2]
+                    parts = (one + two, mixed - one + two)
                     for c, value in enumerate(parts):
                         for t, row, size, k, energy in pieces(energies):
                             if t == tile:
@@ -256,8 +271,8 @@
             for side, start in enumerate((halo, pair_rows)):
                 for k in range(2):
                     for j in range(orb):
-                        row = (j % JBLOCK) * halo
-                        edge[side, k, :, j // JBLOCK, row : row + halo] = ext[
+                        row = (j % PACK) * halo
+                        edge[side, k, :, j // PACK, row : row + halo] = ext[
                             lc, k, irows, j, start : start + halo
                         ]
                 send[lc, side, ib] = edge[side].astype(jnp.bfloat16)
@@ -333,9 +348,9 @@
                 for k in range(2):
                     rows = recv[lc, side, ib, k].astype(jnp.float32) * keep
                     for j in range(orb):
-                        row = (j % JBLOCK) * halo
+                        row = (j % PACK) * halo
                         ext[lc, k, irows, j, start : start + halo] = rows[
-                            :, j // JBLOCK, row : row + halo
+                            :, j // PACK, row : row + halo
                         ]
             totals = list(totals)
             for step in range(IBLOCK):
@@ -444,6 +459,23 @@
         out_copy(k).wait()
 
 
+def copy_kernel(source, small_source, target, small_target, sems):
+    half = source.shape[1] // 2
+    copies = [pltpu.make_async_copy(small_source, small_target, sems.at[4])]
+    for k in range(2):
+        for part in range(2):
+            rows = pl.ds(part * half, half)
+            copies.append(
+                pltpu.make_async_copy(
+                    source.at[k, rows], target.at[k, rows], sems.at[2 * k + part]
+                )
+            )
+    for copy in copies:
+        copy.start()
+    for copy in copies:
+        copy.wait()
+
+
 def local(ne, nz, green_ret, broadening, coupling, occupation, shifts, neighbours, bond_count, bond_weight):
     orb, energies, atoms = green_ret.shape[1], green_ret.shape[3], green_ret.shape[4]
     modes, slots = coupling.shape[0], neighbours.shape[1]
@@ -453,8 +485,8 @@
     tiles = pl.cdiv(pair_rows, ROWS)
     out_rows = ceil_to(pair_rows, ROWS)
     ext_rows = ceil_to(max(pair_rows, out_rows) + 4 * SHIFT, ROWS)
-    iblocks, jblocks = orb // IBLOCK, orb // JBLOCK
-    edge_shape = (2, IBLOCK, jblocks, JBLOCK * 2 * SHIFT, LANES)
+    iblocks = orb // IBLOCK
+    edge_shape = (2, IBLOCK, orb // PACK, PACK * 2 * SHIFT, LANES)
     halo_shape = (chunks, 2, iblocks) + edge_shape
     dma = pltpu.SemaphoreType.DMA
     vmem = pl.BlockSpec(memory_space=pltpu.VMEM)
@@ -475,6 +507,7 @@
             pltpu.VMEM((orb, 2 * pair_rows, LANES), jnp.float32),
             pltpu.VMEM((green_tiles(energies), 4, orb, orb, ROWS, LANES), jnp.float32),
             pltpu.VMEM((tiles, 3, orb, orb, ROWS, LANES), jnp.float32),
+            pltpu.VMEM((3, IBLOCK, JBLOCK, ROWS, LANES), jnp.float32),
             pltpu.VMEM((tiles, 3, IBLOCK, orb, ROWS, LANES), jnp.float32),
             pltpu.VMEM((chunks, 2, orb, orb, ext_rows, LANES), jnp.float32),
             pltpu.VMEM((2,) + edge_shape, jnp.float32),
@@ -518,6 +551,17 @@
         neighbours,
         bond_weight,
     )
+    out, pol = pl.pallas_call(
+        copy_kernel,
+        out_shape=(
+            jax.ShapeDtypeStruct(out.shape, out.dtype),
+            jax.ShapeDtypeStruct(pol.shape, pol.dtype),
+        ),
+        in_specs=[hbm] * 2,
+        out_specs=(hbm, hbm),
+        scratch_shapes=[dma((5,))],
+        compiler_params=pltpu.CompilerParams(vmem_limit_bytes=64 * 1024 * 1024),
+    )(out, pol)
     self_energy = out.reshape(2, orb, orb, energies, 2, atoms).transpose(0, 4, 1, 2, 3, 5)
     return self_energy, pol
 

time: 35.3 us -> 86.7 us (2.46)
  Pallas kernels: 29.9 us -> 85.8 us
  local copies, waits for them, and re-layouts: 4.49 us -> 0 us
    pallas_call x0 -> x1, Pallas kernels: none -> 54.9 us  [local(): pl.pallas_call(copy_kernel, out_shape=(jax.ShapeDtypeStruct(out.shape, ou...]
    unnamed x4 -> x0, local copies, waits for them, and re-layouts: 4.49 us -> none
    pallas_call x1, Pallas kernels: 29.9 us -> 30.9 us  [local(): pl.pallas_call(functools.partial(keldysh_kernel, ne, nz, orb, energies, a...]
where the time goes in v4:
time: 86.7 us; the launch traced here: 86.5 us
  Pallas kernels  85.8 us (99%)
    pallas_call x1, Pallas kernels, local(): pl.pallas_call(copy_kernel, out_shape=(jax.ShapeDtypeStruct(out.shape, ou...  54.9 us
    pallas_call x1, Pallas kernels, local(): pl.pallas_call(functools.partial(keldysh_kernel, ne, nz, orb, energies, a...  30.9 us

profile of v4, /device:TPU:0, one launch (start us, length us, event | category | flops | bytes accessed | tf_op | source)
XLA Modules:
  0.0 86.5 jit_solution(13616559691318600266)
XLA Ops:
  0.6 30.9 %shard_map.95 = (bf16[2,12,288,128]{3,2,1,0:T(8,128)(2,1)}, f32[8,32]{1,0:T(8,128)}) custom-call(bf16[12,288,128]{2,1,0:T(8,128)(2,1)} %bitcast.13, bf16[2,12,288,128]{3,2,1,0:T(8,128)(2,1)} %bitcast.12, f32[1,64]{1,0:T(1,128)} %bitcast.14, f32[1,64]{1,0:T(1,128)} %bitcast.15, s32[1,64]{1,0:T(1,128)} %bitcast.16, s32[32]{0:T(128)} %count_in.1, ...), custom_call_target="tpu_custom_call" | custom-call | tf_op jit(solution)/shard_map/pallas_call | solution.py:496
  31.6 54.9 %shard_map.96 = (bf16[2,12,288,128]{3,2,1,0:T(8,128)(2,1)}, f32[8,32]{1,0:T(8,128)}) custom-call(bf16[2,12,288,128]{3,2,1,0:T(8,128)(2,1)} %get-tuple-element.6.source, f32[8,32]{1,0:T(8,128)} %get-tuple-element.7.small_source), custom_call_target="tpu_custom_call" | custom-call | tf_op jit(solution)/shard_map/pallas_call | solution.py:554

commit v5 on v3

--- a/solution.py
+++ b/solution.py
@@ -12,7 +12,8 @@
 LANES = 128
 ROWS = 8
 IBLOCK = 3
-JBLOCK = 4
+JBLOCK = 3
+PACK = 4
 MESH = pl.DeviceIdType.MESH
 
 
@@ -256,8 +257,8 @@
             for side, start in enumerate((halo, pair_rows)):
                 for k in range(2):
                     for j in range(orb):
-                        row = (j % JBLOCK) * halo
-                        edge[side, k, :, j // JBLOCK, row : row + halo] = ext[
+                        row = (j % PACK) * halo
+                        edge[side, k, :, j // PACK, row : row + halo] = ext[
                             lc, k, irows, j, start : start + halo
                         ]
                 send[lc, side, ib] = edge[side].astype(jnp.bfloat16)
@@ -333,9 +334,9 @@
                 for k in range(2):
                     rows = recv[lc, side, ib, k].astype(jnp.float32) * keep
                     for j in range(orb):
-                        row = (j % JBLOCK) * halo
+                        row = (j % PACK) * halo
                         ext[lc, k, irows, j, start : start + halo] = rows[
-                            :, j // JBLOCK, row : row + halo
+                            :, j // PACK, row : row + halo
                         ]
             totals = list(totals)
             for step in range(IBLOCK):
@@ -444,6 +445,30 @@
         out_copy(k).wait()
 
 
+def copy_kernel(source, small_source, target, small_target, held, small_held, in_sems, out_sems):
+    half = source.shape[1] // 2
+    stages = [(small_source, small_held, small_target)]
+    for k in range(2):
+        for part in range(2):
+            rows = pl.ds(part * half, half)
+            stages.append((source.at[k, rows], held.at[k, rows], target.at[k, rows]))
+    loads = [
+        pltpu.make_async_copy(first, middle, in_sems.at[index])
+        for index, (first, middle, last) in enumerate(stages)
+    ]
+    stores = [
+        pltpu.make_async_copy(middle, last, out_sems.at[index])
+        for index, (first, middle, last) in enumerate(stages)
+    ]
+    for load in loads:
+        load.start()
+    for load, store in zip(loads, stores):
+        load.wait()
+        store.start()
+    for store in stores:
+        store.wait()
+
+
 def local(ne, nz, green_ret, broadening, coupling, occupation, shifts, neighbours, bond_count, bond_weight):
     orb, energies, atoms = green_ret.shape[1], green_ret.shape[3], green_ret.shape[4]
     modes, slots = coupling.shape[0], neighbours.shape[1]
@@ -453,8 +478,8 @@
     tiles = pl.cdiv(pair_rows, ROWS)
     out_rows = ceil_to(pair_rows, ROWS)
     ext_rows = ceil_to(max(pair_rows, out_rows) + 4 * SHIFT, ROWS)
-    iblocks, jblocks = orb // IBLOCK, orb // JBLOCK
-    edge_shape = (2, IBLOCK, jblocks, JBLOCK * 2 * SHIFT, LANES)
+    iblocks = orb // IBLOCK
+    edge_shape = (2, IBLOCK, orb // PACK, PACK * 2 * SHIFT, LANES)
     halo_shape = (chunks, 2, iblocks) + edge_shape
     dma = pltpu.SemaphoreType.DMA
     vmem = pl.BlockSpec(memory_space=pltpu.VMEM)
@@ -518,6 +543,22 @@
         neighbours,
         bond_weight,
     )
+    out, pol = pl.pallas_call(
+        copy_kernel,
+        out_shape=(
+            jax.ShapeDtypeStruct(out.shape, out.dtype),
+            jax.ShapeDtypeStruct(pol.shape, pol.dtype),
+        ),
+        in_specs=[hbm] * 2,
+        out_specs=(hbm, hbm),
+        scratch_shapes=[
+            pltpu.VMEM(out.shape, out.dtype),
+            pltpu.VMEM(pol.shape, pol.dtype),
+            dma((5,)),
+            dma((5,)),
+        ],
+        compiler_params=pltpu.CompilerParams(vmem_limit_bytes=64 * 1024 * 1024),
+    )(out, pol)
     self_energy = out.reshape(2, orb, orb, energies, 2, atoms).transpose(0, 4, 1, 2, 3, 5)
     return self_energy, pol
 

time: 35.3 us -> 33.1 us (0.938)
  local copies, waits for them, and re-layouts: 4.49 us -> 0 us
  Pallas kernels: 29.9 us -> 32.2 us
    unnamed x4 -> x0, local copies, waits for them, and re-layouts: 4.49 us -> none
    pallas_call x0 -> x1, Pallas kernels: none -> 2.3 us  [local(): pl.pallas_call(copy_kernel, out_shape=(jax.ShapeDtypeStruct(out.shape, ou...]
where the time goes in v5:
time: 33.1 us; the launch traced here: 32.8 us
  Pallas kernels  32.2 us (97%)
  between operations  0.64 us (2%)
    pallas_call x1, Pallas kernels, local(): pl.pallas_call(functools.partial(keldysh_kernel, ne, nz, orb, energies, a...  29.9 us
    pallas_call x1, Pallas kernels, local(): pl.pallas_call(copy_kernel, out_shape=(jax.ShapeDtypeStruct(out.shape, ou...  2.3 us

profile of v5, /device:TPU:0, one launch (start us, length us, event | category | flops | bytes accessed | tf_op | source)
XLA Modules:
  0.0 32.8 jit_solution(6828305797181426655)
XLA Ops:
  0.6 29.9 %shard_map.95 = (bf16[2,12,288,128]{3,2,1,0:T(8,128)(2,1)}, f32[8,32]{1,0:T(8,128)}) custom-call(bf16[12,288,128]{2,1,0:T(8,128)(2,1)} %bitcast.13, bf16[2,12,288,128]{3,2,1,0:T(8,128)(2,1)} %bitcast.12, f32[1,64]{1,0:T(1,128)} %bitcast.14, f32[1,64]{1,0:T(1,128)} %bitcast.15, s32[1,64]{1,0:T(1,128)} %bitcast.16, s32[32]{0:T(128)} %count_in.1, ...), custom_call_target="tpu_custom_call" | custom-call | tf_op jit(solution)/shard_map/pallas_call | solution.py:489
  30.5 2.3 %shard_map.96 = (bf16[2,12,288,128]{3,2,1,0:T(8,128)(2,1)}, f32[8,32]{1,0:T(8,128)}) custom-call(bf16[2,12,288,128]{3,2,1,0:T(8,128)(2,1)} %get-tuple-element.6.source, f32[8,32]{1,0:T(8,128)} %get-tuple-element.7.small_source), custom_call_target="tpu_custom_call" | custom-call | tf_op jit(solution)/shard_map/pallas_call | solution.py:546

commit v6 on v5

--- a/solution.py
+++ b/solution.py
@@ -169,7 +169,7 @@
     def green_tile(tile):
         return jnp.where(tile >= repeat, tile - (repeat - edge_tiles), tile)
 
-    def store_forms(target, index, count_of):
+    def store_forms(plain, target, index, count_of):
         for tile in range(target.shape[0]):
             low = tile * ROWS
             size = min(ROWS, pair_rows - low)
@@ -179,7 +179,7 @@
             for form in range(count_of):
                 target[tile, form, index, :, 0:size] = forms[form]
 
-    def spread(blocks, limit):
+    def spread(plain, blocks, limit):
         begin = 0
         for k, start, size in row_plan(energies)[0]:
             if begin < 2 * limit:
@@ -193,21 +193,25 @@
             s_copy.start()
         g_copy.wait()
 
-        @pl.loop(0, orb)
-        def _(i):
-            block = gv[i].astype(jnp.float32).reshape(orb, pair_rows, LANES)
-            spread((block, block), repeat * ROWS)
-            store_forms(gf, i, 4)
+        @pl.loop(0, orb // 2)
+        def _(pair):
+            for slot in range(2):
+                i = 2 * pair + slot
+                block = gv[i].astype(jnp.float32).reshape(orb, pair_rows, LANES)
+                spread(plain.at[slot], (block, block), repeat * ROWS)
+                store_forms(plain.at[slot], gf, i, 4)
 
         s_copy.wait()
 
-        @pl.loop(0, orb)
-        def _(i):
-            spread(
-                [sv[k, i].astype(jnp.float32).reshape(orb, pair_rows, LANES) for k in range(2)],
-                pair_rows,
-            )
-            store_forms(sf, i, 3)
+        @pl.loop(0, orb // 2)
+        def _(pair):
+            for slot in range(2):
+                i = 2 * pair + slot
+                blocks = [
+                    sv[k, i].astype(jnp.float32).reshape(orb, pair_rows, LANES) for k in range(2)
+                ]
+                spread(plain.at[slot], blocks, pair_rows)
+                store_forms(plain.at[slot], sf, i, 3)
 
     def keldysh_chunk(lc):
         if chunks > 1:
@@ -216,7 +220,7 @@
         def products(ib, first_tile, last_tile):
             irows = pl.ds(ib * IBLOCK, IBLOCK)
 
-            @pl.loop(0, (last_tile - first_tile) * jblocks)
+            @pl.loop(0, (last_tile - first_tile) * jblocks, unroll=2)
             def _(step):
                 tile, jb = first_tile + step // jblocks, lax.rem(step, jblocks)
                 jrows = pl.ds(jb * JBLOCK, JBLOCK)
@@ -231,7 +235,7 @@
                 for form, value in enumerate((real, imag, real + imag)):
                     hf[tile, form, :, jrows] = value
 
-            @pl.loop(0, jblocks)
+            @pl.loop(0, jblocks, unroll=2)
             def _(jb):
                 jrows = pl.ds(jb * JBLOCK, JBLOCK)
                 for tile in range(first_tile, last_tile):
@@ -296,7 +300,7 @@
             jnp.zeros((pair_rows - 2 * offset, LANES), jnp.float32)
             for offset in range(1, SHIFT + 1)
         )
-        return lax.fori_loop(0, orb, add_row, starts)
+        return lax.fori_loop(0, orb, add_row, starts, unroll=2)
 
     def signed_sum(total):
         parity = lax.rem(lax.broadcasted_iota(jnp.int32, total.shape, 0), 2)
@@ -382,7 +386,7 @@
     def shift_energies(k):
         upward, downward = (emission, absorption) if k == 0 else (absorption, emission)
 
-        @pl.loop(0, orb)
+        @pl.loop(0, orb, unroll=4)
         def _(i):
             mixed = None
             for lc in range(chunks):
@@ -497,7 +501,7 @@
         scratch_shapes=[
             pltpu.VMEM((orb, orb * pair_rows, LANES), jnp.bfloat16),
             pltpu.VMEM((2, orb, orb * pair_rows, LANES), jnp.bfloat16),
-            pltpu.VMEM((orb, 2 * pair_rows, LANES), jnp.float32),
+            pltpu.VMEM((2, orb, 2 * pair_rows, LANES), jnp.float32),
             pltpu.VMEM((green_tiles(energies), 4, orb, orb, ROWS, LANES), jnp.float32),
             pltpu.VMEM((tiles, 3, orb, orb, ROWS, LANES), jnp.float32),
             pltpu.VMEM((tiles, 3, IBLOCK, orb, ROWS, LANES), jnp.float32),

time: 33.1 us -> 33.1 us (level)
  no operation moved by 1% of the time
where the time goes in v6:
time: 33.1 us; the launch traced here: 32.8 us
  Pallas kernels  32.2 us (97%)
  between operations  0.64 us (2%)
    pallas_call x1, Pallas kernels, local(): pl.pallas_call(functools.partial(keldysh_kernel, ne, nz, orb, energies, a...  29.9 us
    pallas_call x1, Pallas kernels, local(): pl.pallas_call(copy_kernel, out_shape=(jax.ShapeDtypeStruct(out.shape, ou...  2.3 us

profile of v6, /device:TPU:0, one launch (start us, length us, event | category | flops | bytes accessed | tf_op | source)
XLA Modules:
  0.0 32.8 jit_solution(12849178366462648475)
XLA Ops:
  0.6 29.9 %shard_map.95 = (bf16[2,12,288,128]{3,2,1,0:T(8,128)(2,1)}, f32[8,32]{1,0:T(8,128)}) custom-call(bf16[12,288,128]{2,1,0:T(8,128)(2,1)} %bitcast.13, bf16[2,12,288,128]{3,2,1,0:T(8,128)(2,1)} %bitcast.12, f32[1,64]{1,0:T(1,128)} %bitcast.14, f32[1,64]{1,0:T(1,128)} %bitcast.15, s32[1,64]{1,0:T(1,128)} %bitcast.16, s32[32]{0:T(128)} %count_in.1, ...), custom_call_target="tpu_custom_call" | custom-call | tf_op jit(solution)/shard_map/pallas_call | solution.py:493
  30.5 2.3 %shard_map.96 = (bf16[2,12,288,128]{3,2,1,0:T(8,128)(2,1)}, f32[8,32]{1,0:T(8,128)}) custom-call(bf16[2,12,288,128]{3,2,1,0:T(8,128)(2,1)} %get-tuple-element.6.source, f32[8,32]{1,0:T(8,128)} %get-tuple-element.7.small_source), custom_call_target="tpu_custom_call" | custom-call | tf_op jit(solution)/shard_map/pallas_call | solution.py:550
